TPU v7x, 256 devices: a whole 4x4x8 slice. The times are simulated.
256 devices in a mesh: emb: 64 (over z, y, core), seq: 4 (over x).
Axes of the slice: x: 4, y: 4, z: 8, core: 2. Of those that a mesh axis runs over, the one named last changes fastest.
Arguments:
- table: bfloat16 [32768, 256], P('emb'), may hold values from -6 to 6
- owner: int32 [512, 512, 1], P(('emb', 'seq')), may hold values from 0 to 63; in each aligned block of 512 rows (0 to 511, 512 to 1023, ..., all dimensions but the last counted through in order) at most 16 rows name the same one
- row: int32 [512, 512], P(('emb', 'seq')), may hold values from 0 to 511
- conv_weight: float32 [4, 768, 256], replicated, may hold values from -0.21875 to 0.21875
- gain: float32 [4, 256], replicated, may hold values from 0.1 to 1.9
- upstream: bfloat16 [512, 512, 256], P(('emb', 'seq')), may hold values from -6 to 6
Outputs:
- weight_grad: float32 [4, 768, 256], replicated
- gain_grad: float32 [4, 256], replicated
- table_grad: float32 [32768, 256], P('emb')
Inputs may be any that keep to these rules, and one draw needn't show every extreme that they name: Within the positions of one micro-batch on one device (aligned blocks of 512 positions, in sequence order), at most 16 have the same owner.
All inputs are finite; a program needn't handle non-finite values.
Results may differ from a plain program's by a relative error of at most 0.022.
Values may be sent and summed in bfloat16 or wider, within the bound.
A program may use at most 64 MiB of HBM per device.

v0:
```python
import jax
import jax.numpy as jnp
from jax import lax
from jax.sharding import PartitionSpec as P

MB = 2


def shift_back(values, steps):
    return jnp.pad(values, ((0, 0), (steps, 0), (0, 0)))[:, : values.shape[1]]


def shift_ahead(values, steps):
    return jnp.pad(values, ((0, 0), (0, steps), (0, 0)))[:, steps:]


def gelu_tanh(values):
    return jax.nn.gelu(values, approximate=True)


def forward_block(state, weight, gain_row, dilation):
    width = state.shape[-1]
    statef = state.astype(jnp.float32)
    centred = statef - jnp.mean(statef, axis=-1, keepdims=True)
    inverse = lax.rsqrt(jnp.mean(centred * centred, axis=-1, keepdims=True) + 1e-05)
    normed = centred * inverse
    hidden = (normed * gain_row).astype(jnp.bfloat16)
    stacked = jnp.concatenate(
        [hidden, shift_back(hidden, dilation), shift_back(hidden, 2 * dilation)], axis=-1
    )
    flat = stacked.reshape(-1, 3 * width)
    conv = jnp.dot(flat, weight.astype(jnp.bfloat16), preferred_element_type=jnp.float32).reshape(
        state.shape
    )
    result = (statef + gelu_tanh(conv)).astype(jnp.bfloat16)
    return (result, (flat, normed, inverse, conv))


def backward_block(cotangent, saved, weight, gain_row, dilation):
    flat, normed, inverse, conv = saved
    width = cotangent.shape[-1]
    slope = jax.jvp(gelu_tanh, (conv,), (jnp.ones_like(conv),))[1]
    cotf = cotangent.astype(jnp.float32)
    dconv = (cotf * slope).astype(jnp.bfloat16).reshape(-1, width)
    dweight = lax.dot_general(
        flat, dconv, (((0,), (0,)), ((), ())), preferred_element_type=jnp.float32
    )
    dflat = jnp.dot(dconv, weight.astype(jnp.bfloat16).T, preferred_element_type=jnp.float32)
    dflat = dflat.reshape(cotangent.shape[:-1] + (3 * width,))
    dhidden = dflat[..., :width] + shift_ahead(dflat[..., width : 2 * width], dilation)
    dhidden = dhidden + shift_ahead(dflat[..., 2 * width :], 2 * dilation)
    dgain = jnp.sum(dhidden * normed, axis=(0, 1))
    dnorm = dhidden * gain_row
    dstate = inverse * (
        dnorm
        - jnp.mean(dnorm, axis=-1, keepdims=True)
        - normed * jnp.mean(dnorm * normed, axis=-1, keepdims=True)
    )
    return ((cotf + dstate).astype(jnp.bfloat16), dweight, dgain)


def run_stack(embed, weights, gains, cotangent):
    state = embed
    saves = []
    for layer in range(weights.shape[0]):
        state, saved = forward_block(state, weights[layer], gains[layer], 2**layer)
        saves.append(saved)
    weight_parts = []
    gain_parts = []
    for layer in reversed(range(weights.shape[0])):
        cotangent, dweight, dgain = backward_block(
            cotangent, saves[layer], weights[layer], gains[layer], 2**layer
        )
        weight_parts.insert(0, dweight)
        gain_parts.insert(0, dgain)
    return (cotangent, jnp.stack(weight_parts), jnp.stack(gain_parts))


def body(table, owner, row, conv_weight, gain, upstream):
    shards = lax.axis_size("emb")
    seqs_dev, length = row.shape
    slab, width = table.shape
    seq_mb = seqs_dev // MB
    count = seq_mb * length
    capacity = max(2, 2 * count // shards)
    owners = owner.reshape(MB, count)
    marks = (owners[:, :, None] == jnp.arange(shards, dtype=jnp.int32)[None, None, :]).astype(
        jnp.int32
    )
    slots = jnp.sum((jnp.cumsum(marks, axis=1) - 1) * marks, axis=2)
    batch_ids = jnp.broadcast_to(jnp.arange(MB, dtype=jnp.int32)[:, None], (MB, count))
    requests = jnp.zeros((shards, MB, capacity), jnp.int32).at[owners, batch_ids, slots].set(row)
    cotangents = upstream.reshape(MB, seq_mb, length, width)
    weight_total = jnp.zeros(conv_weight.shape, jnp.float32)
    gain_total = jnp.zeros(gain.shape, jnp.float32)
    table_part = jnp.zeros((slab, width), jnp.float32)
    for batch in range(MB):
        arrived_ids = lax.all_to_all(
            requests[:, batch], "emb", split_axis=0, concat_axis=0, tiled=True
        )
        served = table[arrived_ids]
        fetched = lax.all_to_all(served, "emb", split_axis=0, concat_axis=0, tiled=True)
        embed = fetched[owners[batch], slots[batch]].reshape(seq_mb, length, width)
        d_embed, dweight, dgain = run_stack(embed, conv_weight, gain, cotangents[batch])
        weight_total = weight_total + dweight
        gain_total = gain_total + dgain
        outgoing = (
            jnp.zeros((shards, capacity, width), jnp.bfloat16)
            .at[owners[batch], slots[batch]]
            .set(d_embed.reshape(count, width))
        )
        returned = lax.all_to_all(outgoing, "emb", split_axis=0, concat_axis=0, tiled=True)
        table_part = table_part.at[arrived_ids.reshape(-1)].add(
            returned.reshape(-1, width).astype(jnp.float32)
        )
    scale = float(seqs_dev * length * shards * lax.axis_size("seq")) ** (-0.5)
    table_grad = lax.psum(table_part.astype(jnp.bfloat16), "seq").astype(jnp.float32)
    weight_sum, gain_sum = lax.psum((weight_total, gain_total), ("emb", "seq"))
    return (weight_sum * scale, gain_sum * scale, table_grad)


def solution(mesh):
    in_specs = (
        P("emb", None),
        P(("emb", "seq"), None, None),
        P(("emb", "seq"), None),
        P(),
        P(),
        P(("emb", "seq"), None, None),
    )
    out_specs = (P(), P(), P("emb", None))
    return jax.shard_map(body, mesh=mesh, in_specs=in_specs, out_specs=out_specs, check_vma=False)
```

profile of v0, /device:TPU:4, one launch (start us, length us, event | category | flops | bytes accessed | tf_op | source)
XLA Modules:
  0.0 619.9 jit_solution(593469830120721987)
XLA Ops:
  14.5 4.3 scatter_custom_fusion.4
  19.6 12.1 %all-to-all-start.2 = ((s32[64,1,16]{2,1,0:T(1,128)}), s32[64,1,16]{2,1,0:T(1,128)S(1)}, u32[]{:S(2)}, u32[]{:S(2)}) async-start(s32[64,1,16]{2,1,0:T(1,128)} %copy.17), calls=%async_computation.2 | async-start | bytes 65536 | tf_op jit(solution)/shard_map/all_to_all | solution.py:98
  32.4 8.8 %all-to-all-done.2 = s32[64,1,16]{2,1,0:T(1,128)S(1)} async-done(((s32[64,1,16]{2,1,0:T(1,128)}), s32[64,1,16]{2,1,0:T(1,128)S(1)}, u32[]{:S(2)}, u32[]{:S(2)}) %all-to-all-start.2) | async-done | bytes 4128 | tf_op jit(solution)/shard_map/all_to_all | solution.py:98
  41.2 4.6 all-to-all-start
  45.9 5.0 gather_fusion.2
  50.9 4.4 all-to-all-done
  55.3 5.9 all-to-all-start.3
  61.3 5.0 gather_fusion
  66.3 12.6 %all-to-all-done.3 = bf16[64,16,256]{2,1,0:T(8,128)(2,1)S(1)} async-done(((bf16[64,16,256]{2,1,0:T(8,128)(2,1)}), bf16[64,16,256]{2,1,0:T(8,128)(2,1)S(1)}, u32[]{:S(2)}, u32[]{:S(2)}) %all-to-all-start.3) | async-done | bytes 524320 | tf_op jit(solution)/shard_map/all_to_all | solution.py:102
  78.9 6.2 %all-to-all-start.1 = ((bf16[64,16,256]{2,1,0:T(8,128)(2,1)}), bf16[64,16,256]{2,1,0:T(8,128)(2,1)S(1)}, u32[]{:S(2)}, u32[]{:S(2)}) async-start(bf16[64,16,256]{2,1,0:T(8,128)(2,1)} %bitcast.4), calls=%async_computation.1 | async-start | bytes 1048576 | tf_op jit(solution)/shard_map/all_to_all | solution.py:102
  88.6 3.2 gather_fusion.3
  92.2 10.6 %all-to-all-done.1 = bf16[64,16,256]{2,1,0:T(8,128)(2,1)S(1)} async-done(((bf16[64,16,256]{2,1,0:T(8,128)(2,1)}), bf16[64,16,256]{2,1,0:T(8,128)(2,1)S(1)}, u32[]{:S(2)}, u32[]{:S(2)}) %all-to-all-start.1) | async-done | bytes 524320 | tf_op jit(solution)/shard_map/all_to_all | solution.py:102
  102.8 3.2 gather_fusion.1
  131.1 55.8 %scatter_fusion = bf16[64,16,256]{2,1,0:T(8,128)(2,1)} fusion(bf16[64,16,256]{2,1,0:T(8,128)(2,1)} %broadcast.920.clone, s32[512]{0:T(512)S(1)} %bitcast.510, bf16[512,256]{1,0:T(8,128)(2,1)S(1)} %get-tuple-element.97), kind=kCustom, calls=%fused_computation.4 | custom fusion | bytes 790528 | tf_op jit(solution)/shard_map/scatter | solution.py:110
  186.9 5.9 all-to-all-start.4
  194.6 55.8 %scatter_fusion.1 = bf16[64,16,256]{2,1,0:T(8,128)(2,1)} fusion(bf16[64,16,256]{2,1,0:T(8,128)(2,1)} %broadcast.920.clone.1, s32[512]{0:T(512)S(1)} %bitcast.509, bf16[512,256]{1,0:T(8,128)(2,1)S(1)} %get-tuple-element.96), kind=kCustom, calls=%fused_computation.6 | custom fusion | bytes 790528 | tf_op jit(solution)/shard_map/scatter | solution.py:110
  250.3 2.9 convolution_bitcast_fusion.13
  256.4 10.4 %all-to-all-start.5 = ((bf16[64,16,256]{2,1,0:T(8,128)(2,1)}), bf16[64,16,256]{2,1,0:T(8,128)(2,1)S(1)}, u32[]{:S(2)}, u32[]{:S(2)}) async-start(bf16[64,16,256]{2,1,0:T(8,128)(2,1)} %scatter_fusion.1), calls=%async_computation.5 | async-start | bytes 1048576 | tf_op jit(solution)/shard_map/all_to_all | solution.py:112
  275.6 6.3 %scatter_custom_fusion.1 = f32[512,256]{1,0:T(8,128)S(1)} fusion(s32[1024]{0:T(1024)S(1)} %bitcast.543, bf16[1024,256]{1,0:T(8,128)(2,1)S(1)} %bitcast.513, f32[]{:T(128)} %constant.79.clone.1), kind=kCustom, calls=%fused_computation.29 | custom fusion | flops 524288 | bytes 1048580 | tf_op jit(solution)/shard_map/scatter-add | solution.py:113
  284.5 6.3 %scatter_custom_fusion.3 = f32[512,256]{1,0:T(8,128)S(1)} fusion(f32[512,256]{1,0:T(8,128)S(1)} %scatter_custom_fusion.1, s32[1024]{0:T(1024)S(1)} %bitcast.544, bf16[1024,256]{1,0:T(8,128)(2,1)S(1)} %bitcast.514), kind=kCustom, calls=%fused_computation.27 | custom fusion | flops 524288 | bytes 1048576 | tf_op jit(solution)/shard_map/scatter-add | solution.py:113
  291.7 3.7 maximum_add_fusion
  295.5 74.8 %psum.22 = f32[4,256]{1,0:T(4,128)S(1)} all-reduce(f32[4,256]{1,0:T(4,128)S(1)} %maximum_add_fusion.1), channel_id=1, replica_groups=mesh['emb'=64,'seq'=4] {'emb','seq'}, use_global_device_ids=true, to_apply=%region_41.42 | all-reduce | flops 1024 | bytes 8192 | tf_op jit(solution)/shard_map/psum | solution.py:118
  372.7 236.3 %all-reduce.35.cloned.1.call-done = f32[4,768,256]{2,1,0:T(8,128)} async-done(((f32[4,768,256]{2,1,0:T(8,128)}), f32[4,768,256]{2,1,0:T(8,128)}) %all-reduce.35.cloned.1.call-update) | async-done | bytes 3145744 | tf_op jit(solution)/shard_map/psum | solution.py:118
  609.0 3.8 broadcast_multiply_fusion
  (278 shorter events, 56.4 us)
Async XLA Ops:
  7.2 38.8 %copy-start = (bf16[512,256]{1,0:T(8,128)(2,1)S(1)}, bf16[512,256]{1,0:T(8,128)(2,1)}, u32[]{:S(2)}) copy-start(bf16[512,256]{1,0:T(8,128)(2,1)} %param.6) | copy-start | bytes 786436
  19.6 21.6 %all-to-all-start.2 = ((s32[64,1,16]{2,1,0:T(1,128)}), s32[64,1,16]{2,1,0:T(1,128)S(1)}, u32[]{:S(2)}, u32[]{:S(2)}) async-start(s32[64,1,16]{2,1,0:T(1,128)} %copy.17), calls=%async_computation.2 | async-start | bytes 65536 | tf_op jit(solution)/shard_map/all_to_all | solution.py:98
  41.2 14.1 %all-to-all-start = ((s32[64,1,16]{2,1,0:T(1,128)}), s32[64,1,16]{2,1,0:T(1,128)S(1)}, u32[]{:S(2)}, u32[]{:S(2)}) async-start(s32[64,1,16]{2,1,0:T(1,128)} %copy.16), calls=%async_computation | async-start | bytes 65536 | tf_op jit(solution)/shard_map/all_to_all | solution.py:98
  55.3 23.5 %all-to-all-start.3 = ((bf16[64,16,256]{2,1,0:T(8,128)(2,1)}), bf16[64,16,256]{2,1,0:T(8,128)(2,1)S(1)}, u32[]{:S(2)}, u32[]{:S(2)}) async-start(bf16[64,16,256]{2,1,0:T(8,128)(2,1)} %bitcast.45), calls=%async_computation.3 | async-start | bytes 1048576 | tf_op jit(solution)/shard_map/all_to_all | solution.py:102
  61.3 23.8 %copy-start.56 = (f32[4,256]{1,0:T(4,128)S(1)}, f32[4,256]{1,0:T(4,128)}, u32[]{:S(2)}) copy-start(f32[4,256]{1,0:T(4,128)} %param.10) | copy-start | bytes 12292
  78.9 23.9 %all-to-all-start.1 = ((bf16[64,16,256]{2,1,0:T(8,128)(2,1)}), bf16[64,16,256]{2,1,0:T(8,128)(2,1)S(1)}, u32[]{:S(2)}, u32[]{:S(2)}) async-start(bf16[64,16,256]{2,1,0:T(8,128)(2,1)} %bitcast.4), calls=%async_computation.1 | async-start | bytes 1048576 | tf_op jit(solution)/shard_map/all_to_all | solution.py:102
  107.6 20.2 %copy-start.57 = (f32[512,256]{1,0:T(8,128)}, f32[512,256]{1,0:T(8,128)S(1)}, u32[]{:S(2)}) copy-start(f32[512,256]{1,0:T(8,128)S(1)} %get-tuple-element.112) | copy-start | bytes 1572868
  108.8 18.3 %copy-start.61 = (f32[512,256]{1,0:T(8,128)}, f32[512,256]{1,0:T(8,128)S(1)}, u32[]{:S(2)}) copy-start(f32[512,256]{1,0:T(8,128)S(1)} %get-tuple-element.113) | copy-start | bytes 1572868
  110.3 14.1 %copy-start.59 = (f32[512,256]{1,0:T(8,128)}, f32[512,256]{1,0:T(8,128)S(1)}, u32[]{:S(2)}) copy-start(f32[512,256]{1,0:T(8,128)S(1)} %get-tuple-element.114) | copy-start | bytes 1572868
  111.5 12.2 %copy-start.65 = (f32[512,256]{1,0:T(8,128)}, f32[512,256]{1,0:T(8,128)S(1)}, u32[]{:S(2)}) copy-start(f32[512,256]{1,0:T(8,128)S(1)} %get-tuple-element.115) | copy-start | bytes 1572868
  113.0 8.1 %copy-start.63 = (f32[512,256]{1,0:T(8,128)}, f32[512,256]{1,0:T(8,128)S(1)}, u32[]{:S(2)}) copy-start(f32[512,256]{1,0:T(8,128)S(1)} %get-tuple-element.116) | copy-start | bytes 1572868
  114.2 6.2 %copy-start.67 = (f32[512,256]{1,0:T(8,128)}, f32[512,256]{1,0:T(8,128)S(1)}, u32[]{:S(2)}) copy-start(f32[512,256]{1,0:T(8,128)S(1)} %get-tuple-element.117) | copy-start | bytes 1572868
  123.7 2.9 copy-start.18
  186.9 69.5 %all-to-all-start.4 = ((bf16[64,16,256]{2,1,0:T(8,128)(2,1)}), bf16[64,16,256]{2,1,0:T(8,128)(2,1)S(1)}, u32[]{:S(2)}, u32[]{:S(2)}) async-start(bf16[64,16,256]{2,1,0:T(8,128)(2,1)} %scatter_fusion), calls=%async_computation.4 | async-start | bytes 1048576 | tf_op jit(solution)/shard_map/all_to_all | solution.py:112
  194.5 55.8 %copy-start.5 = (bf16[1,512,256]{2,1,0:T(8,128)(2,1)S(1)}, bf16[1,512,256]{2,1,0:T(8,128)(2,1)}, u32[]{:S(2)}) copy-start(bf16[1,512,256]{2,1,0:T(8,128)(2,1)} %copy-done.4) | copy-start | bytes 786436
  194.6 55.8 %copy-start.15 = (bf16[1,512,256]{2,1,0:T(8,128)(2,1)S(1)}, bf16[1,512,256]{2,1,0:T(8,128)(2,1)}, u32[]{:S(2)}) copy-start(bf16[1,512,256]{2,1,0:T(8,128)(2,1)} %copy-done.14) | copy-start | bytes 786436
  254.8 12.1 %copy-start.7 = (bf16[1,512,256]{2,1,0:T(8,128)(2,1)S(1)}, bf16[1,512,256]{2,1,0:T(8,128)(2,1)}, u32[]{:S(2)}) copy-start(bf16[1,512,256]{2,1,0:T(8,128)(2,1)} %copy-done.6) | copy-start | bytes 786436
  254.8 12.1 %copy-start.48 = (bf16[1,512,256]{2,1,0:T(8,128)(2,1)S(1)}, bf16[1,512,256]{2,1,0:T(8,128)(2,1)}, u32[]{:S(2)}) copy-start(bf16[1,512,256]{2,1,0:T(8,128)(2,1)} %copy-done.47) | copy-start | bytes 786436
  256.4 28.1 %all-to-all-start.5 = ((bf16[64,16,256]{2,1,0:T(8,128)(2,1)}), bf16[64,16,256]{2,1,0:T(8,128)(2,1)S(1)}, u32[]{:S(2)}, u32[]{:S(2)}) async-start(bf16[64,16,256]{2,1,0:T(8,128)(2,1)} %scatter_fusion.1), calls=%async_computation.5 | async-start | bytes 1048576 | tf_op jit(solution)/shard_map/all_to_all | solution.py:112
  266.9 104.0 %all-reduce.37.cloned.1.call-start = ((), (), s32[]{:S(2)}) async-start(), calls=%async_computation.7 | async-start | bytes 524288 | tf_op jit(solution)/shard_map/psum | solution.py:117
  275.6 16.1 %copy-start.20 = (f32[1,768,256]{2,1,0:T(8,128)S(1)}, f32[1,768,256]{2,1,0:T(8,128)}, u32[]{:S(2)}) copy-start(f32[1,768,256]{2,1,0:T(8,128)} %convolution_bitcast_fusion.13) | copy-start | bytes 2359300
  281.8 9.8 %copy-start.21 = (f32[1,768,256]{2,1,0:T(8,128)S(1)}, f32[1,768,256]{2,1,0:T(8,128)}, u32[]{:S(2)}) copy-start(f32[1,768,256]{2,1,0:T(8,128)} %convolution_bitcast_fusion.14) | copy-start | bytes 2359300
  291.6 317.3 %all-reduce.35.cloned.1.call-start = ((), (), s32[]{:S(2)}) async-start(), calls=%async_computation.6 | async-start | bytes 6291456 | tf_op jit(solution)/shard_map/psum | solution.py:118
  609.0 3.9 copy-start.1
  (52 other events, 84.8 us)
Sparse Core Ops, SparseCore 0:
  291.8 44.6 all-reduce.36
  343.3 265.5 all-reduce.34
where the time goes:
time: 629 us; the launch traced here: 620 us
  waiting for transfers between devices  275 us (44%)
  local copies, waits for them, and re-layouts  142 us (23%)
  blocking collectives  74.8 us (12%)
  starting transfers between devices  45.3 us (7%)
  other arithmetic  43 us (7%)
  matrix products  23.5 us (4%)
  between operations  15.6 us (2%)
    psum x1, waiting for transfers between devices, body(): weight_sum, gain_sum = lax.psum((weight_total, gain_total), ('emb', 'seq'))  236 us
    scatter x2, local copies, waits for them, and re-layouts, body(): outgoing = jnp.zeros((shards, capacity, width), jnp.bfloat16).at[owners[b...  112 us
    psum x1, blocking collectives, body(): weight_sum, gain_sum = lax.psum((weight_total, gain_total), ('emb', 'seq'))  74.8 us
    all_to_all x2, waiting for transfers between devices, body(): lax.all_to_all(served, 'emb', split_axis=0, concat_axis=0, tiled=True)  23.2 us
    all_to_all x2, starting transfers between devices, body(): lax.all_to_all(requests[:, batch], 'emb', split_axis=0, concat_axis=0, ti...  16.7 us
    all_to_all x2, starting transfers between devices, body(): lax.all_to_all(outgoing, 'emb', split_axis=0, concat_axis=0, tiled=True)  16.4 us
    dot_general x8, matrix products, backward_block(): lax.dot_general(flat, dconv, (((0,), (0,)), ((), ())), preferred_element_...  14.4 us
    all_to_all x2, waiting for transfers between devices, body(): lax.all_to_all(requests[:, batch], 'emb', split_axis=0, concat_axis=0, ti...  13.2 us
  transfers between devices with their start and end apart: 8, of which 6 were waited for; matrix products, arithmetic and copies ran while one was open for 16% of the time, Pallas kernels for 0%

commit v1 on v0

v1 whole, which is shorter than its diff:
```python
import functools
import math

import jax
import jax.numpy as jnp
from jax import lax
from jax.experimental import pallas as pl
from jax.experimental.pallas import tpu as pltpu
from jax.sharding import PartitionSpec as P

MB = 2
CAP = 16
LANES = 128
F32 = jnp.float32
BF16 = jnp.bfloat16
I32 = jnp.int32
NT = (((1,), (1,)), ((), ()))
TN = (((0,), (0,)), ((), ()))


def plan(shards, seq_axis):
    core = 2
    y = 4 if shards >= 64 else 2
    return shards // (core * y), y, core, seq_axis


def iota(shape, axis):
    return lax.broadcasted_iota(I32, shape, axis)


def dot(a, b, dims=(((1,), (0,)), ((), ()))):
    return lax.dot_general(a, b, dims, preferred_element_type=F32)


def whole(ref, sem):
    pltpu.make_async_copy(ref, ref, sem).wait()


def greet(peers):
    barrier = pltpu.get_barrier_semaphore()
    total = 0
    for count, device in peers:

        def hello(k, carry, device=device):
            pl.semaphore_signal(barrier, inc=1, device_id=device(k), device_id_type=pl.DeviceIdType.MESH)
            return carry

        lax.fori_loop(0, count, hello, 0)
        total += count
    pl.semaphore_wait(barrier, total)


def scatter_to(count, device, src, dst, send_sem, recv_sem):
    def step(k, carry):
        pltpu.make_async_remote_copy(
            src_ref=src(k),
            dst_ref=dst,
            send_sem=send_sem,
            recv_sem=recv_sem,
            device_id=device(k),
            device_id_type=pl.DeviceIdType.MESH,
        ).start()
        return carry

    lax.fori_loop(0, count, step, 0)


def emb_peer(shards):
    me, x = lax.axis_index("emb"), lax.axis_index("seq")

    def index(k):
        return lax.rem(me + k + 1, shards)

    return index, lambda k: (index(k), x)


def requests(owner, row, shards, lane0):
    tokens = owner.shape[1]
    named = iota((shards, tokens), 0) == owner
    marks = jnp.where(named, 1.0, 0.0).astype(F32)
    upto = jnp.where(iota((tokens, tokens), 0) <= iota((tokens, tokens), 1), 1.0, 0.0).astype(BF16)
    ranks = dot(marks.astype(BF16), upto)
    slot = jnp.sum(marks * ranks, axis=0, keepdims=True).astype(I32) - 1
    high = (row // 16).astype(F32)
    low = (row % 16).astype(F32)
    values = jnp.concatenate([marks * high, marks * low], axis=0).astype(BF16)
    places = jnp.where(iota((LANES, tokens), 0) == slot + lane0, 1.0, 0.0).astype(BF16)
    wanted = dot(values, places, NT)
    wanted = wanted[:shards] * 16.0 + wanted[shards:]
    return owner * CAP + slot, wanted.astype(I32)


def fetch_kernel(shards, seq_axis, owner_ref, row_ref, table_ref, embed_ref, q_ref, ids_ref,
                 ask, asked, serve, fetched, send_sem, recv_sem):
    tokens = row_ref.shape[1]
    rows = table_ref.shape[0]
    me = lax.axis_index("emb")
    index, device = emb_peer(shards)
    groups = shards // 8
    greet([(shards - 1, device)])
    lane0 = lax.rem(me, 8) * CAP
    places = []
    for m in range(MB):
        q, wanted = requests(owner_ref[m : m + 1, :], row_ref[m : m + 1, :], shards, lane0)
        q_ref[m : m + 1, :] = q
        ask[:, m, :] = wanted
        places.append(q)
    mine = pltpu.make_async_copy(ask.at[me], asked.at[me], recv_sem.at[0])
    mine.start()
    scatter_to(shards - 1, device, lambda k: ask.at[index(k)], asked.at[me], send_sem.at[0], recv_sem.at[0])
    whole(asked, recv_sem.at[0])
    for m in range(MB):
        ids = jnp.sum(asked[:, m, :].reshape(groups, 8, LANES), axis=1)
        ids_ref[m] = ids
        tall = jnp.concatenate([ids.astype(F32)] * (LANES // groups), axis=0).T
        for g in range(groups):
            hot = jnp.where(iota((LANES, rows), 1).astype(F32) == tall[:, g : g + 1], 1.0, 0.0).astype(BF16)
            serve[m, g * LANES : (g + 1) * LANES, :] = dot(hot, table_ref[...]).astype(BF16)
        sem = 1 + m
        here = pl.ds(pl.multiple_of(me * CAP, CAP), CAP)
        pltpu.make_async_copy(serve.at[m, here], fetched.at[m, here], recv_sem.at[sem]).start()
        scatter_to(
            shards - 1,
            device,
            lambda k, m=m: serve.at[m, pl.ds(pl.multiple_of(index(k) * CAP, CAP), CAP)],
            fetched.at[m, here],
            send_sem.at[sem],
            recv_sem.at[sem],
        )
    for m in range(MB):
        whole(fetched.at[m], recv_sem.at[1 + m])
        column = jnp.broadcast_to(places[m].astype(F32), (LANES, tokens)).T
        slots = shards * CAP
        hot = jnp.concatenate(
            [
                jnp.where(column == (iota((tokens, LANES), 1) + s).astype(F32), 1.0, 0.0).astype(BF16)
                for s in range(0, slots, LANES)
            ],
            axis=1,
        )
        embed_ref[m] = dot(hot, fetched[m]).astype(BF16)
    whole(ask.at[pl.ds(0, shards - 1)], send_sem.at[0])
    for m in range(MB):
        whole(serve.at[m, pl.ds(0, (shards - 1) * CAP)], send_sem.at[1 + m])


def block_kernel(chunk, embed_ref, weight_ref, gain_ref, up_ref, grad_ref, dweight_ref, dgain_ref,
                 wide, padded, conv, normed, inverse, slope, hidden, dwide):
    layers, taps, width = weight_ref.shape
    tokens = embed_ref.shape[1]
    top = padded.shape[0] - tokens
    pad = top // 2
    for l in range(layers):
        wide[l] = weight_ref[l].astype(BF16)
    padded[0:pad, :] = jnp.zeros((pad, width), F32)
    padded[pad + tokens :, :] = jnp.zeros((pad, width), F32)
    spans = [slice(c, c + chunk) for c in range(0, tokens, chunk)]
    inv_width = 1.0 / width
    k0 = math.sqrt(2.0 / math.pi)
    for m in range(MB):
        for l in range(layers):
            d = 2**l
            if l == 0:
                source = lambda at: embed_ref[m, at, :].astype(F32)
            gain = gain_ref[l : l + 1, :]
            for at in spans:
                if l == 0:
                    state = embed_ref[m, at, :].astype(F32)
                else:
                    state = normed[m, l, at, :]
                centred = state - jnp.sum(state, axis=-1, keepdims=True) * inv_width
                rstd = lax.rsqrt(jnp.sum(centred * centred, axis=-1, keepdims=True) * inv_width + 1e-05)
                norm = centred * rstd
                if l < layers - 1:
                    normed[m, l + 1, at, :] = state
                normed[m, l, at, :] = norm
                inverse[m, l, at, :] = jnp.broadcast_to(rstd, (chunk, LANES))
                padded[pad + at.start : pad + at.stop, :] = norm * gain
            for k in range(3):
                for at in spans:
                    moved = padded[pad + at.start - k * d : pad + at.stop - k * d, :]
                    hidden[m, l, at, k * width : (k + 1) * width] = moved.astype(BF16)
            conv[...] = dot(hidden[m, l], wide[l])
            for at in spans:
                c = conv[at, :]
                c2 = c * c
                t = jnp.tanh(c * (k0 + (k0 * 0.044715) * c2))
                half = 0.5 + 0.5 * t
                slope[m, l, at, :] = half + c * (0.5 - 0.5 * t * t) * (k0 + (3 * k0 * 0.044715) * c2)
                if l < layers - 1:
                    state = normed[m, l + 1, at, :]
                    normed[m, l + 1, at, :] = (state + c * half).astype(BF16).astype(F32)
    for m in range(MB):
        for l in reversed(range(layers)):
            d = 2**l
            gain = gain_ref[l : l + 1, :]
            src = up_ref if l == layers - 1 else grad_ref
            for at in spans:
                padded[pad + at.start : pad + at.stop, :] = src[m, at, :].astype(F32) * slope[m, l, at, :]
            for k in range(3):
                for at in spans:
                    moved = padded[pad + at.start + k * d : pad + at.stop + k * d, :]
                    dwide[m, at, k * width : (k + 1) * width] = moved.astype(BF16)
            for k in range(3):
                part = dot(hidden[m, l, :, 0:width], dwide[m, :, k * width : (k + 1) * width], TN)
                rows = slice(k * width, (k + 1) * width)
                if m == 0:
                    dweight_ref[l, rows, :] = part
                else:
                    dweight_ref[l, rows, :] += part
            dh = dot(dwide[m, :, 0:width], wide[l, 0:width, :], NT)
            dh = dh + dot(dwide[m, :, width : 2 * width], wide[l, width : 2 * width, :], NT)
            dh = dh + dot(dwide[m, :, 2 * width :], wide[l, 2 * width :, :], NT)
            conv[...] = dh
            dgain = jnp.zeros((1, width), F32)
            for at in spans:
                dh = conv[at, :]
                norm = normed[m, l, at, :]
                both = dh * norm
                dgain = dgain + jnp.sum(both, axis=0, keepdims=True)
                dn = dh * gain
                m1 = jnp.sum(dn, axis=-1, keepdims=True) * inv_width
                m2 = jnp.sum(both * gain, axis=-1, keepdims=True) * inv_width
                rstd = inverse[m, l, at, 0:1]
                grad_ref[m, at, :] = (
                    src[m, at, :].astype(F32) + rstd * (dn - m1 - norm * m2)
                ).astype(BF16)
            if m == 0:
                dgain_ref[l : l + 1, :] = dgain
            else:
                dgain_ref[l : l + 1, :] += dgain


def return_kernel(shards, seq_axis, scale, grad_ref, q_ref, ids_ref, dweight_ref, dgain_ref,
                  weight_out, gain_out, table_out,
                  back, returned, tsend, trecv, tall_recv,
                  s0, r0, s1, r1, r2, r3, r4, g0, g1, g2, send_sem, recv_sem, wsend, wrecv):
    z_size, y_size, _, x_size = plan(shards, seq_axis)
    layers, taps, width = dweight_ref.shape
    tokens = grad_ref.shape[1]
    rows = table_out.shape[0]
    slots = shards * CAP
    e, x = lax.axis_index("emb"), lax.axis_index("seq")
    c = lax.rem(e, 2)
    y = lax.rem(e // 2, y_size)
    z = e // (2 * y_size)
    plane = x_size * y_size
    p_me = x * y_size + y
    index, device = emb_peer(shards)
    sibling = (e + 1 - 2 * c, x)

    def x_index(k):
        return lax.rem(x + k + 1, x_size)

    def x_device(k):
        return (e, x_index(k))

    def p_index(k):
        return lax.rem(p_me + k + 1, plane)

    def p_device(k):
        p = p_index(k)
        return ((z * y_size + lax.rem(p, y_size)) * 2 + c, p // y_size)

    def z_device(k):
        return ((lax.rem(z + k + 1, z_size) * y_size + y) * 2 + c, x)

    def off_device(k):
        py = lax.rem(y + 1 + lax.rem(k, y_size - 1), y_size)
        px = lax.rem(x + 1 + k // (y_size - 1), x_size)
        return ((z * y_size + py) * 2 + c, px)

    greet([(shards - 1, device), (x_size - 1, x_device), ((x_size - 1) * (y_size - 1), off_device)])

    here = pl.ds(pl.multiple_of(e * CAP, CAP), CAP)
    for m in range(MB):
        for s in range(0, slots, LANES):
            hot = jnp.where(iota((LANES, tokens), 0) + s == q_ref[m : m + 1, :], 1.0, 0.0).astype(BF16)
            back[m, s : s + LANES, :] = dot(hot, grad_ref[m]).astype(BF16)
        pltpu.make_async_copy(back.at[m, here], returned.at[m, here], recv_sem.at[m]).start()
        scatter_to(
            shards - 1,
            device,
            lambda k, m=m: back.at[m, pl.ds(pl.multiple_of(index(k) * CAP, CAP), CAP)],
            returned.at[m, here],
            send_sem.at[m],
            recv_sem.at[m],
        )

    half = taps // 2
    blocks = plane // 2
    high = half // blocks

    def remote(src, dst, send, recv, to):
        return pltpu.make_async_remote_copy(
            src_ref=src, dst_ref=dst, send_sem=send, recv_sem=recv, device_id=to, device_id_type=pl.DeviceIdType.MESH
        )

    theirs = pl.ds(pl.multiple_of((1 - c) * half, half), half)
    ours = pl.ds(pl.multiple_of(c * half, half), half)
    for l in range(layers):
        s0[l] = dweight_ref[l, theirs, :].astype(BF16)
        remote(s0.at[l], r0.at[l], wsend.at[0, l], wrecv.at[0, l], sibling).start()
    g0[0] = jnp.concatenate([dgain_ref[...], jnp.zeros_like(dgain_ref)], axis=0)
    gain_pair = remote(g0.at[0], g0.at[1], wsend.at[0, layers], wrecv.at[0, layers], sibling)
    gain_pair.start()
    for l in range(layers):
        whole(r0.at[l], wrecv.at[0, l])
        total = dweight_ref[l, ours, :] + r0[l].astype(F32)
        for b in range(blocks):
            for h in range(2):
                s1[l, b * 2 + h] = total[b * high : (b + 1) * high, h * LANES : (h + 1) * LANES].astype(BF16)
        pltpu.make_async_copy(s1.at[l, p_me], r1.at[l, p_me], wrecv.at[1, l]).start()
        scatter_to(plane - 1, p_device, lambda k, l=l: s1.at[l, p_index(k)], r1.at[l, p_me], wsend.at[1, l], wrecv.at[1, l])
    gain_pair.wait_recv()
    g1[p_me] = g0[0] + g0[1]
    scatter_to(plane - 1, p_device, lambda k: g1.at[p_me], g1.at[p_me], wsend.at[1, layers], wrecv.at[1, layers])
    for l in range(layers):
        whole(r1.at[l], wrecv.at[1, l])
        total = jnp.zeros((high, LANES), F32)
        for p in range(plane):
            total = total + r1[l, p].astype(F32)
        r2[l, z] = total.astype(BF16)
        scatter_to(z_size - 1, z_device, lambda k, l=l: r2.at[l, z], r2.at[l, z], wsend.at[2, l], wrecv.at[2, l])
    whole(g1.at[pl.ds(0, plane - 1)], wrecv.at[1, layers])
    whole(g1.at[pl.ds(0, plane - 1)], wsend.at[1, layers])
    total = g1[0]
    for p in range(1, plane):
        total = total + g1[p]
    g2[z] = total
    scatter_to(z_size - 1, z_device, lambda k: g2.at[z], g2.at[z], wsend.at[2, layers], wrecv.at[2, layers])
    for l in range(layers):
        whole(r2.at[l, pl.ds(0, z_size - 1)], wrecv.at[2, l])
        total = r2[l, 0].astype(F32)
        for k in range(1, z_size):
            total = total + r2[l, k].astype(F32)
        r3[l, p_me] = total.astype(BF16)
        scatter_to(plane - 1, p_device, lambda k, l=l: r3.at[l, p_me], r3.at[l, p_me], wsend.at[3, l], wrecv.at[3, l])
    for l in range(layers):
        whole(r3.at[l, pl.ds(0, plane - 1)], wrecv.at[3, l])
        remote(r3.at[l], r4.at[l], wsend.at[4, l], wrecv.at[4, l], sibling).start()

    part = jnp.zeros((rows, width), F32)
    for m in range(MB):
        whole(returned.at[m], recv_sem.at[m])
        hot = jnp.concatenate(
            [
                jnp.where(iota((rows, LANES), 0) == ids_ref[m, g : g + 1, :], 1.0, 0.0).astype(BF16)
                for g in range(slots // LANES)
            ],
            axis=1,
        )
        part = part + dot(hot, returned[m])
    piece = rows // x_size
    tsend[...] = part.astype(BF16).reshape(x_size, piece, width)
    pltpu.make_async_copy(tsend.at[x], trecv.at[x], recv_sem.at[2]).start()
    scatter_to(x_size - 1, x_device, lambda k: tsend.at[x_index(k)], trecv.at[x], send_sem.at[2], recv_sem.at[2])
    whole(trecv, recv_sem.at[2])
    total = trecv[0].astype(F32)
    for k in range(1, x_size):
        total = total + trecv[k].astype(F32)
    tall_recv[x] = total.astype(BF16)
    scatter_to(x_size - 1, x_device, lambda k: tall_recv.at[x], tall_recv.at[x], send_sem.at[3], recv_sem.at[3])

    whole(g2.at[pl.ds(0, z_size - 1)], wrecv.at[2, layers])
    total = g2[0]
    for k in range(1, z_size):
        total = total + g2[k]
    gain_out[...] = total[:layers] * scale
    for l in range(layers):
        whole(r4.at[l], wrecv.at[4, l])
        for b in range(blocks):
            for h in range(2):
                cols = slice(h * LANES, (h + 1) * LANES)
                weight_out[l, pl.ds(pl.multiple_of(c * half + b * high, 8), high), cols] = r3[l, b * 2 + h].astype(F32) * scale
                weight_out[l, pl.ds(pl.multiple_of((1 - c) * half + b * high, 8), high), cols] = (
                    r4[l, b * 2 + h].astype(F32) * scale
                )
    whole(tall_recv.at[pl.ds(0, x_size - 1)], recv_sem.at[3])
    table_out[...] = tall_recv[...].astype(F32).reshape(rows, width)

    for m in range(MB):
        whole(back.at[m, pl.ds(0, slots - CAP)], send_sem.at[m])
    whole(tsend.at[pl.ds(0, x_size - 1)], send_sem.at[2])
    whole(tsend.at[pl.ds(0, x_size - 1)], send_sem.at[3])
    for l in range(layers):
        whole(s0.at[l], wsend.at[0, l])
        whole(s1.at[l, pl.ds(0, plane - 1)], wsend.at[1, l])
        whole(r2.at[l, pl.ds(0, z_size - 1)], wsend.at[2, l])
        whole(r3.at[l, pl.ds(0, plane - 1)], wsend.at[3, l])
        whole(r3.at[l], wsend.at[4, l])
    gain_pair.wait_send()
    whole(g2.at[pl.ds(0, z_size - 1)], wsend.at[2, layers])


def vmem(count):
    return [pl.BlockSpec(memory_space=pltpu.VMEM)] * count


def body(table, owner, row, conv_weight, gain, upstream):
    shards, seq_axis = lax.axis_size("emb"), lax.axis_size("seq")
    _, tokens = row.shape
    rows, width = table.shape
    layers, taps, _ = conv_weight.shape
    slots = shards * CAP
    z_size, y_size, _, x_size = plan(shards, seq_axis)
    plane = x_size * y_size
    limit = 56 * 2**20
    shape = jax.ShapeDtypeStruct
    dma = pltpu.SemaphoreType.DMA
    embed, q, ids = pl.pallas_call(
        functools.partial(fetch_kernel, shards, seq_axis),
        out_shape=[
            shape((MB, tokens, width), BF16),
            shape((MB, tokens), I32),
            shape((MB, shards // 8, LANES), I32),
        ],
        in_specs=vmem(3),
        out_specs=vmem(3),
        scratch_shapes=[
            pltpu.VMEM((shards, MB, LANES), I32),
            pltpu.VMEM((shards, MB, LANES), I32),
            pltpu.VMEM((MB, slots, width), BF16),
            pltpu.VMEM((MB, slots, width), BF16),
            dma((3,)),
            dma((3,)),
        ],
        compiler_params=pltpu.CompilerParams(collective_id=0, has_side_effects=True, vmem_limit_bytes=limit),
    )(owner.reshape(MB, tokens), row, table)
    chunk = 64
    grad, dweight, dgain = pl.pallas_call(
        functools.partial(block_kernel, chunk),
        out_shape=[
            shape((MB, tokens, width), BF16),
            shape((layers, taps, width), F32),
            shape((layers, width), F32),
        ],
        in_specs=vmem(4),
        out_specs=vmem(3),
        scratch_shapes=[
            pltpu.VMEM((layers, taps, width), BF16),
            pltpu.VMEM((tokens + 32, width), F32),
            pltpu.VMEM((tokens, width), F32),
            pltpu.VMEM((MB, layers, tokens, width), F32),
            pltpu.VMEM((MB, layers, tokens, LANES), F32),
            pltpu.VMEM((MB, layers, tokens, width), F32),
            pltpu.VMEM((MB, layers, tokens, taps), BF16),
            pltpu.VMEM((MB, tokens, taps), BF16),
        ],
        compiler_params=pltpu.CompilerParams(vmem_limit_bytes=limit),
    )(embed, conv_weight, gain, upstream)
    half = taps // 2
    high = half // (plane // 2)
    piece = rows // x_size
    scale = float(MB * tokens * shards * seq_axis) ** (-0.5)
    return pl.pallas_call(
        functools.partial(return_kernel, shards, seq_axis, scale),
        out_shape=[
            shape((layers, taps, width), F32),
            shape((layers, width), F32),
            shape((rows, width), F32),
        ],
        in_specs=vmem(5),
        out_specs=vmem(3),
        scratch_shapes=[
            pltpu.VMEM((MB, slots, width), BF16),
            pltpu.VMEM((MB, slots, width), BF16),
            pltpu.VMEM((x_size, piece, width), BF16),
            pltpu.VMEM((x_size, piece, width), BF16),
            pltpu.VMEM((x_size, piece, width), BF16),
            pltpu.VMEM((layers, half, width), BF16),
            pltpu.VMEM((layers, half, width), BF16),
            pltpu.VMEM((layers, plane, high, LANES), BF16),
            pltpu.VMEM((layers, plane, high, LANES), BF16),
            pltpu.VMEM((layers, z_size, high, LANES), BF16),
            pltpu.VMEM((layers, plane, high, LANES), BF16),
            pltpu.VMEM((layers, plane, high, LANES), BF16),
            pltpu.VMEM((2, 2 * layers, width), F32),
            pltpu.VMEM((plane, 2 * layers, width), F32),
            pltpu.VMEM((z_size, 2 * layers, width), F32),
            dma((4,)),
            dma((4,)),
            dma((5, layers + 1)),
            dma((5, layers + 1)),
        ],
        compiler_params=pltpu.CompilerParams(collective_id=1, has_side_effects=True, vmem_limit_bytes=limit),
    )(grad, q, ids, dweight, dgain)


def solution(mesh):
    in_specs = (
        P("emb", None),
        P(("emb", "seq"), None, None),
        P(("emb", "seq"), None),
        P(),
        P(),
        P(("emb", "seq"), None, None),
    )
    out_specs = (P(), P(), P("emb", None))
    return jax.shard_map(body, mesh=mesh, in_specs=in_specs, out_specs=out_specs, check_vma=False)
```

time: 629 us -> 130 us (0.21); the launches traced: 620 us -> 128 us
  waiting for transfers between devices: 275 us -> 0 us
  local copies, waits for them, and re-layouts: 142 us -> 6.49 us
  Pallas kernels: 0 us -> 121 us
  blocking collectives: 74.8 us -> 0 us
  starting transfers between devices: 45.3 us -> 0 us
  other arithmetic: 43 us -> 0 us
  matrix products: 23.5 us -> 0 us
  between operations: 15.6 us -> 0.67 us
    psum x2 -> x0, waiting for transfers between devices: 236 us -> none  [the longest x1 236 us: body(): weight_sum, gain_sum = lax.psum((weight_total, gain_total), ('emb', 'seq'))]
    pallas_call x0 -> x3, Pallas kernels: none -> 121 us  [the longest x1 60.2 us: body(): pl.pallas_call(functools.partial(return_kernel, shards, seq_axis, scale),...]
    scatter x2 -> x0, local copies, waits for them, and re-layouts: 112 us -> none  [body(): outgoing = jnp.zeros((shards, capacity, width), jnp.bfloat16).at[owners[b...]
    psum x1 -> x0, blocking collectives: 74.8 us -> none  [body(): weight_sum, gain_sum = lax.psum((weight_total, gain_total), ('emb', 'seq'))]
    all_to_all x6 -> x0, starting transfers between devices: 45.2 us -> none  [the longest x2 16.7 us: body(): lax.all_to_all(requests[:, batch], 'emb', split_axis=0, concat_axis=0, ti...]
    all_to_all x6 -> x0, waiting for transfers between devices: 39.1 us -> none  [the longest x2 23.2 us: body(): lax.all_to_all(served, 'emb', split_axis=0, concat_axis=0, tiled=True)]
    dot_general x24 -> x0, matrix products: 23.5 us -> none  [the longest x8 14.4 us: backward_block(): lax.dot_general(flat, dconv, (((0,), (0,)), ((), ())), preferred_element_...]
    gather x4 -> x0, local copies, waits for them, and re-layouts: 16.3 us -> none  [the longest x2 9.97 us: body(): served = table[arrived_ids]]
  transfers between devices with their start and end apart: 8 -> 0, of which waited for: 6 -> 0; matrix products, arithmetic and copies ran while one was open for 16% -> 0% of each run, Pallas kernels for 0% -> 0%
where the time goes in v1:
time: 130 us; the launch traced here: 128 us
  Pallas kernels  121 us (93%)
  local copies, waits for them, and re-layouts  6.49 us (5%)
    pallas_call x1, Pallas kernels, body(): pl.pallas_call(functools.partial(return_kernel, shards, seq_axis, scale),...  60.2 us
    pallas_call x1, Pallas kernels, body(): pl.pallas_call(functools.partial(fetch_kernel, shards, seq_axis), out_sha...  45.9 us
    pallas_call x1, Pallas kernels, body(): pl.pallas_call(functools.partial(block_kernel, chunk), out_shape=[shape((...  15.1 us
    unnamed x8, local copies, waits for them, and re-layouts  6.49 us

profile of v1, /device:TPU:4, one launch (start us, length us, event | category | flops | bytes accessed | tf_op | source)
XLA Modules:
  0.0 128.3 jit_solution(5368324431781244787)
XLA Ops:
  0.6 1.3 copy.11
  1.9 45.9 %shard_map.85 = (bf16[2,512,256]{2,1,0:T(8,128)(2,1)}, s32[2,512]{1,0:T(2,128)}, s32[2,8,128]{2,1,0:T(8,128)}) custom-call(s32[2,512]{1,0:T(2,128)} %bitcast.3, s32[2,512]{1,0:T(2,128)} %row_ref.1, bf16[512,256]{1,0:T(8,128)(2,1)} %table_ref.1), custom_call_target="tpu_custom_call" | custom-call | tf_op jit(solution)/shard_map/pallas_call | solution.py:411
  47.8 15.1 %shard_map.86 = (bf16[2,512,256]{2,1,0:T(8,128)(2,1)}, f32[4,768,256]{2,1,0:T(8,128)}, f32[4,256]{1,0:T(4,128)}) custom-call(bf16[2,512,256]{2,1,0:T(8,128)(2,1)} %get-tuple-element.9.embed_ref, f32[4,768,256]{2,1,0:T(8,128)} %weight_ref.1, f32[4,256]{1,0:T(4,128)} %gain_ref.1, bf16[2,512,256]{2,1,0:T(8,128)(2,1)} %up_ref.1), custom_call_target="tpu_custom_call" | custom-call | tf_op jit(solution)/shard_map/pallas_call | solution.py:431
  62.9 60.2 %shard_map.87 = (f32[4,768,256]{2,1,0:T(8,128)}, f32[4,256]{1,0:T(4,128)}, f32[512,256]{1,0:T(8,128)}) custom-call(bf16[2,512,256]{2,1,0:T(8,128)(2,1)} %get-tuple-element.10.grad_ref, s32[2,512]{1,0:T(2,128)} %get-tuple-element.11.q_ref, s32[2,8,128]{2,1,0:T(8,128)} %get-tuple-element.12.ids_ref, f32[4,768,256]{2,1,0:T(8,128)} %get-tuple-element.13.dweight_ref, ...), custom_call_target="tpu_custom_call" | custom-call | tf_op jit(solution)/shard_map/pallas_call | solution.py:456
  123.1 0.0 copy-start.1
  123.1 0.0 copy-start
  123.1 3.8 %copy.15 = f32[4,768,256]{2,1,0:T(8,128)} copy(f32[4,768,256]{2,1,0:T(8,128)} %get-tuple-element.18) | data formatting | bytes 6291456
  126.9 0.0 copy-done.1
  127.0 0.6 copy.16
  127.5 0.0 copy-done
  127.5 0.8 copy.17
Async XLA Ops:
  123.1 3.8 %copy-start.1 = (f32[4,256]{1,0:T(4,128)S(1)}, f32[4,256]{1,0:T(4,128)}, u32[]{:S(2)}) copy-start(f32[4,256]{1,0:T(4,128)} %get-tuple-element.19) | copy-start | bytes 12292
  123.1 4.4 %copy-start = (f32[512,256]{1,0:T(8,128)S(1)}, f32[512,256]{1,0:T(8,128)}, u32[]{:S(2)}) copy-start(f32[512,256]{1,0:T(8,128)} %get-tuple-element.20) | copy-start | bytes 1572868

commit v2 on v0

v2 whole, which is shorter than its diff:
```python
import functools
import math

import jax
import jax.numpy as jnp
from jax import lax
from jax.experimental import pallas as pl
from jax.experimental.pallas import tpu as pltpu
from jax.sharding import PartitionSpec as P

MB = 2
CAP = 16
LANES = 128
F32 = jnp.float32
BF16 = jnp.bfloat16
I32 = jnp.int32
NT = (((1,), (1,)), ((), ()))
TN = (((0,), (0,)), ((), ()))


def plan(shards, seq_axis):
    core = 2
    y = 4 if shards >= 64 else 2
    return shards // (core * y), y, core, seq_axis


def iota(shape, axis):
    return lax.broadcasted_iota(I32, shape, axis)


def dot(a, b, dims=(((1,), (0,)), ((), ()))):
    return lax.dot_general(a, b, dims, preferred_element_type=F32)


def whole(ref, sem):
    pltpu.make_async_copy(ref, ref, sem).wait()


def greet(peers):
    barrier = pltpu.get_barrier_semaphore()
    total = 0
    for count, device in peers:

        def hello(k, carry, device=device):
            pl.semaphore_signal(barrier, inc=1, device_id=device(k), device_id_type=pl.DeviceIdType.MESH)
            return carry

        lax.fori_loop(0, count, hello, 0)
        total += count
    return total


def scatter_to(count, device, src, dst, send_sem, recv_sem):
    def step(k, carry):
        pltpu.make_async_remote_copy(
            src_ref=src(k),
            dst_ref=dst,
            send_sem=send_sem,
            recv_sem=recv_sem,
            device_id=device(k),
            device_id_type=pl.DeviceIdType.MESH,
        ).start()
        return carry

    lax.fori_loop(0, count, step, 0)


def emb_peer(shards):
    me, x = lax.axis_index("emb"), lax.axis_index("seq")

    def index(k):
        return lax.rem(me + k + 1, shards)

    return index, lambda k: (index(k), x)


def requests(owner, row, shards, lane0):
    tokens = owner.shape[1]
    named = iota((shards, tokens), 0) == owner
    marks = jnp.where(named, 1.0, 0.0).astype(F32)
    upto = jnp.where(iota((tokens, tokens), 0) <= iota((tokens, tokens), 1), 1.0, 0.0).astype(BF16)
    ranks = dot(marks.astype(BF16), upto)
    slot = jnp.sum(marks * ranks, axis=0, keepdims=True).astype(I32) - 1
    high = (row // 16).astype(F32)
    low = (row % 16).astype(F32)
    values = jnp.concatenate([marks * high, marks * low], axis=0).astype(BF16)
    places = jnp.where(iota((LANES, tokens), 0) == slot + lane0, 1.0, 0.0).astype(BF16)
    wanted = dot(values, places, NT)
    wanted = wanted[:shards] * 16.0 + wanted[shards:]
    return owner * CAP + slot, wanted.astype(I32)


def window_kernel(shards, seq_axis, chunk,
                  owner_ref, row_ref, table_ref, gain_ref, weight_hbm, up_hbm,
                  weight_out, gain_out, table_out,
                  ask, asked, serve, fetched, back, returned, pick, place, add,
                  weight_ref, up_ref, wide, padded, conv, normed, inverse, slope, hidden, dwide, grad_ref,
                  dweight_ref, tsend, trecv, s0, r0, s1, r1, r2, r3, g0, g1, g2,
                  load_sem, send_sem, recv_sem, wsend, wrecv):
    z_size, y_size, _, x_size = plan(shards, seq_axis)
    layers, taps, width = weight_ref.shape
    tokens = row_ref.shape[1]
    rows = table_ref.shape[0]
    slots = shards * CAP
    groups = shards // 8
    e, x = lax.axis_index("emb"), lax.axis_index("seq")
    c = lax.rem(e, 2)
    y = lax.rem(e // 2, y_size)
    z = e // (2 * y_size)
    plane = x_size * y_size
    p_me = x * y_size + y
    index, device = emb_peer(shards)
    sibling = (e + 1 - 2 * c, x)
    half = taps // 2
    high = half // (plane // 2)
    batches = 2
    deep = layers // batches

    def x_index(k):
        return lax.rem(x + k + 1, x_size)

    def x_device(k):
        return (e, x_index(k))

    def p_index(k):
        return lax.rem(p_me + k + 1, plane)

    def p_device(k):
        p = p_index(k)
        return ((z * y_size + lax.rem(p, y_size)) * 2 + c, p // y_size)

    def z_device(k):
        return ((lax.rem(z + k + 1, z_size) * y_size + y) * 2 + c, x)

    def off_device(k):
        py = lax.rem(y + 1 + lax.rem(k, y_size - 1), y_size)
        px = lax.rem(x + 1 + k // (y_size - 1), x_size)
        return ((z * y_size + py) * 2 + c, px)

    def remote(src, dst, send, recv, to):
        return pltpu.make_async_remote_copy(
            src_ref=src, dst_ref=dst, send_sem=send, recv_sem=recv, device_id=to, device_id_type=pl.DeviceIdType.MESH
        )

    load_weight = pltpu.make_async_copy(weight_hbm, weight_ref, load_sem.at[0])
    load_up = pltpu.make_async_copy(up_hbm, up_ref, load_sem.at[1])
    load_weight.start()
    load_up.start()
    expected = greet([(shards - 1, device), (x_size - 1, x_device), ((x_size - 1) * (y_size - 1), off_device)])

    lane0 = lax.rem(e, 8) * CAP
    places = []
    for m in range(MB):
        q, wanted = requests(owner_ref[m], row_ref[m : m + 1, :], shards, lane0)
        ask[:, m, :] = wanted
        places.append(q)
    pl.semaphore_wait(pltpu.get_barrier_semaphore(), expected)
    pltpu.make_async_copy(ask.at[e], asked.at[e], recv_sem.at[0]).start()
    scatter_to(shards - 1, device, lambda k: ask.at[index(k)], asked.at[e], send_sem.at[0], recv_sem.at[0])

    for m in range(MB):
        column = jnp.broadcast_to(places[m].astype(F32), (LANES, tokens)).T
        for s in range(0, slots, LANES):
            pick[m, :, s : s + LANES] = jnp.where(
                column == (iota((tokens, LANES), 1) + s).astype(F32), 1.0, 0.0
            ).astype(BF16)
            place[m, s : s + LANES, :] = jnp.where(iota((LANES, tokens), 0) + s == places[m], 1.0, 0.0).astype(BF16)
    load_weight.wait()
    for l in range(layers):
        wide[l] = weight_ref[l].astype(BF16)
    pad = (padded.shape[0] - tokens) // 2
    padded[0:pad, :] = jnp.zeros((pad, width), F32)
    padded[pad + tokens :, :] = jnp.zeros((pad, width), F32)

    here = pl.ds(pl.multiple_of(e * CAP, CAP), CAP)
    whole(asked, recv_sem.at[0])
    wanted = []
    for m in range(MB):
        ids = jnp.sum(asked[:, m, :].reshape(groups, 8, LANES), axis=1)
        wanted.append(ids)
        tall = jnp.concatenate([ids.astype(F32)] * (LANES // groups), axis=0).T
        for g in range(groups):
            hot = jnp.where(iota((LANES, rows), 1).astype(F32) == tall[:, g : g + 1], 1.0, 0.0).astype(BF16)
            serve[m, g * LANES : (g + 1) * LANES, :] = dot(hot, table_ref[...]).astype(BF16)
        pltpu.make_async_copy(serve.at[m, here], fetched.at[m, here], recv_sem.at[1 + m]).start()
        scatter_to(
            shards - 1,
            device,
            lambda k, m=m: serve.at[m, pl.ds(pl.multiple_of(index(k) * CAP, CAP), CAP)],
            fetched.at[m, here],
            send_sem.at[1 + m],
            recv_sem.at[1 + m],
        )
    for m in range(MB):
        for g in range(groups):
            add[m, :, g * LANES : (g + 1) * LANES] = jnp.where(
                iota((rows, LANES), 0) == wanted[m][g : g + 1, :], 1.0, 0.0
            ).astype(BF16)
    load_up.wait()

    spans = [slice(at, at + chunk) for at in range(0, tokens, chunk)]
    inv_width = 1.0 / width
    k0 = math.sqrt(2.0 / math.pi)

    def forward(m):
        conv[...] = dot(pick[m], fetched[m])
        for l in range(layers):
            d = 2**l
            gain = gain_ref[l : l + 1, :]
            for at in spans:
                if l == 0:
                    state = conv[at, :]
                else:
                    state = normed[m, l, at, :]
                centred = state - jnp.sum(state, axis=-1, keepdims=True) * inv_width
                rstd = lax.rsqrt(jnp.sum(centred * centred, axis=-1, keepdims=True) * inv_width + 1e-05)
                norm = centred * rstd
                if l < layers - 1:
                    normed[m, l + 1, at, :] = state
                normed[m, l, at, :] = norm
                inverse[m, l, at, :] = jnp.broadcast_to(rstd, (chunk, LANES))
                padded[pad + at.start : pad + at.stop, :] = norm * gain
            for k in range(3):
                for at in spans:
                    moved = padded[pad + at.start - k * d : pad + at.stop - k * d, :]
                    hidden[m, l, at, k * width : (k + 1) * width] = moved.astype(BF16)
            conv[...] = dot(hidden[m, l], wide[l])
            for at in spans:
                v = conv[at, :]
                v2 = v * v
                t = jnp.tanh(v * (k0 + (k0 * 0.044715) * v2))
                side = 0.5 + 0.5 * t
                slope[m, l, at, :] = side + v * (0.5 - 0.5 * t * t) * (k0 + (3 * k0 * 0.044715) * v2)
                if l < layers - 1:
                    state = normed[m, l + 1, at, :]
                    normed[m, l + 1, at, :] = (state + v * side).astype(BF16).astype(F32)

    def backward(m, after):
        for l in reversed(range(layers)):
            d = 2**l
            gain = gain_ref[l : l + 1, :]
            src = up_ref if l == layers - 1 else grad_ref
            for at in spans:
                padded[pad + at.start : pad + at.stop, :] = src[m, at, :].astype(F32) * slope[m, l, at, :]
            for k in range(3):
                for at in spans:
                    moved = padded[pad + at.start + k * d : pad + at.stop + k * d, :]
                    dwide[m, at, k * width : (k + 1) * width] = moved.astype(BF16)
            for k in range(3):
                part = dot(hidden[m, l, :, 0:width], dwide[m, :, k * width : (k + 1) * width], TN)
                taken = slice(k * width, (k + 1) * width)
                if m == 0:
                    dweight_ref[l, taken, :] = part
                else:
                    dweight_ref[l, taken, :] += part
            dh = dot(dwide[m, :, 0:width], wide[l, 0:width, :], NT)
            dh = dh + dot(dwide[m, :, width : 2 * width], wide[l, width : 2 * width, :], NT)
            dh = dh + dot(dwide[m, :, 2 * width :], wide[l, 2 * width :, :], NT)
            conv[...] = dh
            dgain = jnp.zeros((1, width), F32)
            for at in spans:
                dh = conv[at, :]
                norm = normed[m, l, at, :]
                both = dh * norm
                dgain = dgain + jnp.sum(both, axis=0, keepdims=True)
                dn = dh * gain
                m1 = jnp.sum(dn, axis=-1, keepdims=True) * inv_width
                m2 = jnp.sum(both * gain, axis=-1, keepdims=True) * inv_width
                rstd = inverse[m, l, at, 0:1]
                grad_ref[m, at, :] = (
                    src[m, at, :].astype(F32) + rstd * (dn - m1 - norm * m2)
                ).astype(BF16)
            if m == 0:
                g0[0, l : l + 1, :] = dgain
            else:
                g0[0, l : l + 1, :] += dgain
            after(l)

    def send_back(m):
        for s in range(0, slots, LANES):
            back[m, s : s + LANES, :] = dot(place[m, s : s + LANES, :], grad_ref[m]).astype(BF16)
        pltpu.make_async_copy(back.at[m, here], returned.at[m, here], recv_sem.at[3 + m]).start()
        scatter_to(
            shards - 1,
            device,
            lambda k: back.at[m, pl.ds(pl.multiple_of(index(k) * CAP, CAP), CAP)],
            returned.at[m, here],
            send_sem.at[3 + m],
            recv_sem.at[3 + m],
        )

    theirs = pl.ds(pl.multiple_of((1 - c) * half, half), half)
    ours = pl.ds(pl.multiple_of(c * half, half), half)

    def halves(l):
        s0[l] = dweight_ref[l, theirs, :].astype(BF16)
        if l % deep == 0:
            b = l // deep
            remote(s0.at[pl.ds(l, deep)], r0.at[pl.ds(l, deep)], wsend.at[0, b], wrecv.at[0, b], sibling).start()

    whole(fetched.at[0], recv_sem.at[1])
    forward(0)
    g0[0] = jnp.zeros_like(g0[0])
    backward(0, lambda l: None)
    send_back(0)
    whole(fetched.at[1], recv_sem.at[2])
    forward(1)
    backward(1, halves)
    send_back(1)

    last = batches
    gain_pair = remote(g0.at[0], g0.at[1], wsend.at[0, last], wrecv.at[0, last], sibling)
    gain_pair.start()

    def piece(p):
        return (
            pl.ds(pl.multiple_of((p // 2) * high, 16), high),
            pl.ds(pl.multiple_of(lax.rem(p, 2) * LANES, LANES), LANES),
        )

    def out_piece(p):
        return (
            pl.ds(pl.multiple_of(c * half + (p // 2) * high, 16), high),
            pl.ds(pl.multiple_of(lax.rem(p, 2) * LANES, LANES), LANES),
        )

    order = list(reversed(range(batches)))
    for b in order:
        at = pl.ds(b * deep, deep)
        whole(r0.at[at], wrecv.at[0, b])
        for l in range(b * deep, (b + 1) * deep):
            s1[l] = (dweight_ref[l, ours, :] + r0[l].astype(F32)).astype(BF16)
        pltpu.make_async_copy(s1.at[(at, *piece(p_me))], r1.at[b, p_me], wrecv.at[1, b]).start()
        scatter_to(
            plane - 1,
            p_device,
            lambda k, at=at: s1.at[(at, *piece(p_index(k)))],
            r1.at[b, p_me],
            wsend.at[1, b],
            wrecv.at[1, b],
        )
    gain_pair.wait_recv()
    g1[p_me] = g0[0] + g0[1]
    scatter_to(plane - 1, p_device, lambda k: g1.at[p_me], g1.at[p_me], wsend.at[1, last], wrecv.at[1, last])
    for b in order:
        whole(r1.at[b], wrecv.at[1, b])
        total = r1[b, 0].astype(F32)
        for p in range(1, plane):
            total = total + r1[b, p].astype(F32)
        r2[b, z] = total.astype(BF16)
        scatter_to(z_size - 1, z_device, lambda k, b=b: r2.at[b, z], r2.at[b, z], wsend.at[2, b], wrecv.at[2, b])
    whole(g1.at[pl.ds(0, plane - 1)], wrecv.at[1, last])
    whole(g1.at[pl.ds(0, plane - 1)], wsend.at[1, last])
    total = g1[0]
    for p in range(1, plane):
        total = total + g1[p]
    g2[z] = total
    scatter_to(z_size - 1, z_device, lambda k: g2.at[z], g2.at[z], wsend.at[2, last], wrecv.at[2, last])
    whole(returned.at[0], recv_sem.at[3])
    conv[...] = dot(add[0], returned[0])
    for b in order:
        at = pl.ds(b * deep, deep)
        whole(r2.at[b, pl.ds(0, z_size - 1)], wrecv.at[2, b])
        total = r2[b, 0].astype(F32)
        for k in range(1, z_size):
            total = total + r2[b, k].astype(F32)
        r3[b] = total.astype(BF16)
        mine = weight_out.at[(at, *out_piece(p_me))]
        pltpu.make_async_copy(r3.at[b], mine, wrecv.at[3, b]).start()
        scatter_to(plane - 1, p_device, lambda k, b=b: r3.at[b], mine, wsend.at[3, b], wrecv.at[3, b])

    share = rows // x_size
    whole(returned.at[1], recv_sem.at[4])
    tsend[...] = (conv[0:rows, :] + dot(add[1], returned[1])).astype(BF16).reshape(x_size, share, width)
    pltpu.make_async_copy(tsend.at[x], trecv.at[x], recv_sem.at[5]).start()
    scatter_to(x_size - 1, x_device, lambda k: tsend.at[x_index(k)], trecv.at[x], send_sem.at[5], recv_sem.at[5])

    for b in order:
        at = pl.ds(b * deep, deep)
        done = weight_out.at[at, ours]
        whole(done, wrecv.at[3, b])
        remote(done, done, wsend.at[4, b], wrecv.at[4, b], sibling).start()

    whole(trecv, recv_sem.at[5])
    total = trecv[0].astype(F32)
    for k in range(1, x_size):
        total = total + trecv[k].astype(F32)
    table_out[x] = total.astype(BF16)
    scatter_to(x_size - 1, x_device, lambda k: table_out.at[x], table_out.at[x], send_sem.at[6], recv_sem.at[6])

    whole(g2.at[pl.ds(0, z_size - 1)], wrecv.at[2, last])
    total = g2[0]
    for k in range(1, z_size):
        total = total + g2[k]
    gain_out[...] = total[:layers]
    for b in order:
        whole(weight_out.at[pl.ds(b * deep, deep), theirs], wrecv.at[4, b])
    whole(table_out.at[pl.ds(0, x_size - 1)], recv_sem.at[6])

    whole(ask.at[pl.ds(0, shards - 1)], send_sem.at[0])
    for m in range(MB):
        whole(serve.at[m, pl.ds(0, slots - CAP)], send_sem.at[1 + m])
        whole(back.at[m, pl.ds(0, slots - CAP)], send_sem.at[3 + m])
    whole(tsend.at[pl.ds(0, x_size - 1)], send_sem.at[5])
    whole(tsend.at[pl.ds(0, x_size - 1)], send_sem.at[6])
    for b in range(batches):
        at = pl.ds(b * deep, deep)
        whole(s0.at[at], wsend.at[0, b])
        whole(r1.at[b, pl.ds(0, plane - 1)], wsend.at[1, b])
        whole(r2.at[b, pl.ds(0, z_size - 1)], wsend.at[2, b])
        whole(r1.at[b, pl.ds(0, plane - 1)], wsend.at[3, b])
        whole(weight_out.at[at, ours], wsend.at[4, b])
    gain_pair.wait_send()
    whole(g2.at[pl.ds(0, z_size - 1)], wsend.at[2, last])


def body(table, owner, row, conv_weight, gain, upstream):
    shards, seq_axis = lax.axis_size("emb"), lax.axis_size("seq")
    _, tokens = row.shape
    rows, width = table.shape
    layers, taps, _ = conv_weight.shape
    slots = shards * CAP
    z_size, y_size, _, x_size = plan(shards, seq_axis)
    plane = x_size * y_size
    shape = jax.ShapeDtypeStruct
    dma = pltpu.SemaphoreType.DMA
    half = taps // 2
    high = half // (plane // 2)
    share = rows // x_size
    near = pl.BlockSpec(memory_space=pltpu.VMEM)
    far = pl.BlockSpec(memory_space=pl.ANY)
    weight_sum, gain_sum, table_grad = pl.pallas_call(
        functools.partial(window_kernel, shards, seq_axis, 64),
        out_shape=[
            shape((layers, taps, width), BF16),
            shape((layers, width), F32),
            shape((x_size, share, width), BF16),
        ],
        in_specs=[near, near, near, near, far, far],
        out_specs=[near, near, near],
        scratch_shapes=[
            pltpu.VMEM((shards, MB, LANES), I32),
            pltpu.VMEM((shards, MB, LANES), I32),
            pltpu.VMEM((MB, slots, width), BF16),
            pltpu.VMEM((MB, slots, width), BF16),
            pltpu.VMEM((MB, slots, width), BF16),
            pltpu.VMEM((MB, slots, width), BF16),
            pltpu.VMEM((MB, tokens, slots), BF16),
            pltpu.VMEM((MB, slots, tokens), BF16),
            pltpu.VMEM((MB, rows, slots), BF16),
            pltpu.VMEM((layers, taps, width), F32),
            pltpu.VMEM((MB, tokens, width), BF16),
            pltpu.VMEM((layers, taps, width), BF16),
            pltpu.VMEM((tokens + 32, width), F32),
            pltpu.VMEM((max(tokens, rows), width), F32),
            pltpu.VMEM((MB, layers, tokens, width), F32),
            pltpu.VMEM((MB, layers, tokens, LANES), F32),
            pltpu.VMEM((MB, layers, tokens, width), F32),
            pltpu.VMEM((MB, layers, tokens, taps), BF16),
            pltpu.VMEM((MB, tokens, taps), BF16),
            pltpu.VMEM((MB, tokens, width), BF16),
            pltpu.VMEM((layers, taps, width), F32),
            pltpu.VMEM((x_size, share, width), BF16),
            pltpu.VMEM((x_size, share, width), BF16),
            pltpu.VMEM((layers, half, width), BF16),
            pltpu.VMEM((layers, half, width), BF16),
            pltpu.VMEM((layers, half, width), BF16),
            pltpu.VMEM((2, plane, layers // 2, high, LANES), BF16),
            pltpu.VMEM((2, z_size, layers // 2, high, LANES), BF16),
            pltpu.VMEM((2, layers // 2, high, LANES), BF16),
            pltpu.VMEM((2, 2 * layers, width), F32),
            pltpu.VMEM((plane, 2 * layers, width), F32),
            pltpu.VMEM((z_size, 2 * layers, width), F32),
            dma((2,)),
            dma((7,)),
            dma((7,)),
            dma((5, 3)),
            dma((5, 3)),
        ],
        compiler_params=pltpu.CompilerParams(
            collective_id=0, has_side_effects=True, vmem_limit_bytes=60 * 2**20
        ),
    )(owner.reshape(MB, 1, tokens), row, table, gain, conv_weight, upstream)
    scale = float(MB * tokens * shards * seq_axis) ** (-0.5)
    return weight_sum.astype(F32) * scale, gain_sum * scale, table_grad.astype(F32).reshape(rows, width)


def solution(mesh):
    in_specs = (
        P("emb", None),
        P(("emb", "seq"), None, None),
        P(("emb", "seq"), None),
        P(),
        P(),
        P(("emb", "seq"), None, None),
    )
    out_specs = (P(), P(), P("emb", None))
    return jax.shard_map(body, mesh=mesh, in_specs=in_specs, out_specs=out_specs, check_vma=False)
```

time: 629 us -> 104 us (0.17); the launches traced: 620 us -> 102 us
  waiting for transfers between devices: 275 us -> 0 us
  local copies, waits for them, and re-layouts: 142 us -> 0.01 us
  Pallas kernels: 0 us -> 96.6 us
  blocking collectives: 74.8 us -> 0 us
  starting transfers between devices: 45.3 us -> 0 us
  other arithmetic: 43 us -> 4.82 us
  matrix products: 23.5 us -> 0 us
  between operations: 15.6 us -> 0.66 us
    psum x2 -> x0, waiting for transfers between devices: 236 us -> none  [the longest x1 236 us: body(): weight_sum, gain_sum = lax.psum((weight_total, gain_total), ('emb', 'seq'))]
    scatter x2 -> x0, local copies, waits for them, and re-layouts: 112 us -> none  [body(): outgoing = jnp.zeros((shards, capacity, width), jnp.bfloat16).at[owners[b...]
    pallas_call x0 -> x1, Pallas kernels: none -> 96.6 us  [body(): pl.pallas_call(functools.partial(window_kernel, shards, seq_axis, 64), ou...]
    psum x1 -> x0, blocking collectives: 74.8 us -> none  [body(): weight_sum, gain_sum = lax.psum((weight_total, gain_total), ('emb', 'seq'))]
    all_to_all x6 -> x0, starting transfers between devices: 45.2 us -> none  [the longest x2 16.7 us: body(): lax.all_to_all(requests[:, batch], 'emb', split_axis=0, concat_axis=0, ti...]
    all_to_all x6 -> x0, waiting for transfers between devices: 39.1 us -> none  [the longest x2 23.2 us: body(): lax.all_to_all(served, 'emb', split_axis=0, concat_axis=0, tiled=True)]
    dot_general x24 -> x0, matrix products: 23.5 us -> none  [the longest x8 14.4 us: backward_block(): lax.dot_general(flat, dconv, (((0,), (0,)), ((), ())), preferred_element_...]
    gather x4 -> x0, local copies, waits for them, and re-layouts: 16.3 us -> none  [the longest x2 9.97 us: body(): served = table[arrived_ids]]
  transfers between devices with their start and end apart: 8 -> 0, of which waited for: 6 -> 0; matrix products, arithmetic and copies ran while one was open for 16% -> 0% of each run, Pallas kernels for 0% -> 0%
where the time goes in v2:
time: 104 us; the launch traced here: 102 us
  Pallas kernels  96.6 us (93%)
  other arithmetic  4.82 us (5%)
    pallas_call x1, Pallas kernels, body(): pl.pallas_call(functools.partial(window_kernel, shards, seq_axis, 64), ou...  96.6 us
    mul x1, other arithmetic, body(): weight_sum.astype(F32) * scale  3.38 us

profile of v2, /device:TPU:4, one launch (start us, length us, event | category | flops | bytes accessed | tf_op | source)
XLA Modules:
  0.0 102.1 jit_solution(17671072993330731446)
XLA Ops:
  0.6 96.6 %shard_map.85 = (bf16[4,768,256]{2,1,0:T(8,128)(2,1)}, f32[4,256]{1,0:T(4,128)}, bf16[4,128,256]{2,1,0:T(8,128)(2,1)}) custom-call(s32[2,1,512]{2,1,0:T(1,128)} %bitcast.4, s32[2,512]{1,0:T(2,128)} %row_ref.1, bf16[512,256]{1,0:T(8,128)(2,1)} %table_ref.1, f32[4,256]{1,0:T(4,128)} %gain_ref.1, f32[4,768,256]{2,1,0:T(8,128)} %weight_hbm.1, ...), custom_call_target="tpu_custom_call" | custom-call | tf_op jit(solution)/shard_map/pallas_call | solution.py:432
  97.2 0.0 copy-start
  97.2 0.0 copy-start.1
  97.3 3.4 %convert_multiply_fusion = f32[4,768,256]{2,1,0:T(8,128)} fusion(bf16[4,768,256]{2,1,0:T(8,128)(2,1)} %get-tuple-element.6), kind=kLoop, calls=%fused_computation | loop fusion | flops 1572864 | bytes 4718592 | tf_op jit(solution)/shard_map/mul | solution.py:485
  100.6 0.0 copy-done
  100.6 0.8 bitcast_convert_fusion
  101.5 0.0 copy-done.1
  101.5 0.6 broadcast_multiply_fusion
Async XLA Ops:
  97.2 3.4 %copy-start = (bf16[4,128,256]{2,1,0:T(8,128)(2,1)S(1)}, bf16[4,128,256]{2,1,0:T(8,128)(2,1)}, u32[]{:S(2)}) copy-start(bf16[4,128,256]{2,1,0:T(8,128)(2,1)} %get-tuple-element.8) | copy-start | bytes 786436
  97.2 4.2 %copy-start.1 = (f32[4,256]{1,0:T(4,128)S(1)}, f32[4,256]{1,0:T(4,128)}, u32[]{:S(2)}) copy-start(f32[4,256]{1,0:T(4,128)} %get-tuple-element.7) | copy-start | bytes 12292

commit v3 on v2

--- a/solution.py
+++ b/solution.py
@@ -72,6 +72,39 @@
         return lax.rem(me + k + 1, shards)
 
     return index, lambda k: (index(k), x)
+
+
+def to_emb(sizes, src, dst, send_sem, recv_sem, rounds=None):
+    z_size, y_size, core, _ = sizes
+    line = y_size * core
+    me, x = lax.axis_index("emb"), lax.axis_index("seq")
+    c, y, z = lax.rem(me, core), lax.rem(me // core, y_size), me // line
+    steps = sorted(range(-((z_size - 1) // 2), z_size // 2 + 1), key=lambda d: (-abs(d), -d))
+    levels = [lax.rem(z + d + z_size, z_size) * line for d in steps]
+
+    def send(level, near):
+        peer = level + near
+        pltpu.make_async_remote_copy(
+            src_ref=src(peer),
+            dst_ref=dst,
+            send_sem=send_sem,
+            recv_sem=recv_sem,
+            device_id=(peer, x),
+            device_id_type=pl.DeviceIdType.MESH,
+        ).start()
+
+    def step(j, carry):
+        k = line - 1 - j
+        near = lax.rem(y + k // core, y_size) * core + lax.rem(c + k, core)
+        for level in levels:
+            send(level, near)
+        return carry
+
+    first, last = rounds or (0, line)
+    lax.fori_loop(first, min(last, line - 1), step, 0)
+    if last == line:
+        for level in levels[:-1]:
+            send(level, y * core + c)
 
 
 def requests(owner, row, shards, lane0):
@@ -90,14 +123,30 @@
     return owner * CAP + slot, wanted.astype(I32)
 
 
+DURING = {0: [(0, 0)], 1: [(0, 1), (1, 0)], 2: [(1, 1), (2, 0)], 3: [(2, 1), (3, 0), (0, 2)]}
+AFTER = [
+    [(3, 1), (1, 2)],
+    [(2, 2), (0, 3)],
+    [(3, 2), (1, 3), (2, 3)],
+    [(0, 4), (3, 3), (1, 4)],
+]
+LATE = [(2, 4), (3, 4), (0, 5), (1, 5)]
+LAST = [(2, 5), (3, 5)]
+
+
+def batches_of(layers):
+    return [(l, 1) for l in reversed(range(layers))]
+
+
 def window_kernel(shards, seq_axis, chunk,
                   owner_ref, row_ref, table_ref, gain_ref, weight_hbm, up_hbm,
                   weight_out, gain_out, table_out,
                   ask, asked, serve, fetched, back, returned, pick, place, add,
                   weight_ref, up_ref, wide, padded, conv, normed, inverse, slope, hidden, dwide, grad_ref,
-                  dweight_ref, tsend, trecv, s0, r0, s1, r1, r2, r3, g0, g1, g2,
-                  load_sem, send_sem, recv_sem, wsend, wrecv):
-    z_size, y_size, _, x_size = plan(shards, seq_axis)
+                  dweight_ref, tsend, trecv, s0, r0, s1, g0, g1, g2, g3,
+                  load_sem, send_sem, recv_sem, wsend, wrecv, *work):
+    sizes = plan(shards, seq_axis)
+    z_size, y_size, _, x_size = sizes
     layers, taps, width = weight_ref.shape
     tokens = row_ref.shape[1]
     rows = table_ref.shape[0]
@@ -107,20 +156,27 @@
     c = lax.rem(e, 2)
     y = lax.rem(e // 2, y_size)
     z = e // (2 * y_size)
+    _, device = emb_peer(shards)
+    sibling = (e + 1 - 2 * c, x)
+    half = taps // 2
+    sets = batches_of(layers)
+    count = len(sets)
+    r1, s2, r2, t2, r3 = (work[k * count : (k + 1) * count] for k in range(5))
     plane = x_size * y_size
     p_me = x * y_size + y
-    index, device = emb_peer(shards)
-    sibling = (e + 1 - 2 * c, x)
-    half = taps // 2
     high = half // (plane // 2)
-    batches = 2
-    deep = layers // batches
 
     def x_index(k):
         return lax.rem(x + k + 1, x_size)
 
     def x_device(k):
         return (e, x_index(k))
+
+    def y_index(k):
+        return lax.rem(y + k + 1, y_size)
+
+    def y_device(k):
+        return ((z * y_size + y_index(k)) * 2 + c, x)
 
     def p_index(k):
         return lax.rem(p_me + k + 1, plane)
@@ -128,14 +184,17 @@
     def p_device(k):
         p = p_index(k)
         return ((z * y_size + lax.rem(p, y_size)) * 2 + c, p // y_size)
-
-    def z_device(k):
-        return ((lax.rem(z + k + 1, z_size) * y_size + y) * 2 + c, x)
 
     def off_device(k):
         py = lax.rem(y + 1 + lax.rem(k, y_size - 1), y_size)
         px = lax.rem(x + 1 + k // (y_size - 1), x_size)
         return ((z * y_size + py) * 2 + c, px)
+
+    def z_index(k):
+        return lax.rem(z + k + 1, z_size)
+
+    def z_device(k):
+        return ((z_index(k) * y_size + y) * 2 + c, x)
 
     def remote(src, dst, send, recv, to):
         return pltpu.make_async_remote_copy(
@@ -156,7 +215,7 @@
         places.append(q)
     pl.semaphore_wait(pltpu.get_barrier_semaphore(), expected)
     pltpu.make_async_copy(ask.at[e], asked.at[e], recv_sem.at[0]).start()
-    scatter_to(shards - 1, device, lambda k: ask.at[index(k)], asked.at[e], send_sem.at[0], recv_sem.at[0])
+    to_emb(sizes, lambda peer: ask.at[peer], asked.at[e], send_sem.at[0], recv_sem.at[0])
 
     for m in range(MB):
         column = jnp.broadcast_to(places[m].astype(F32), (LANES, tokens)).T
@@ -183,10 +242,9 @@
             hot = jnp.where(iota((LANES, rows), 1).astype(F32) == tall[:, g : g + 1], 1.0, 0.0).astype(BF16)
             serve[m, g * LANES : (g + 1) * LANES, :] = dot(hot, table_ref[...]).astype(BF16)
         pltpu.make_async_copy(serve.at[m, here], fetched.at[m, here], recv_sem.at[1 + m]).start()
-        scatter_to(
-            shards - 1,
-            device,
-            lambda k, m=m: serve.at[m, pl.ds(pl.multiple_of(index(k) * CAP, CAP), CAP)],
+        to_emb(
+            sizes,
+            lambda peer, m=m: serve.at[m, pl.ds(pl.multiple_of(peer * CAP, CAP), CAP)],
             fetched.at[m, here],
             send_sem.at[1 + m],
             recv_sem.at[1 + m],
@@ -276,125 +334,144 @@
                 g0[0, l : l + 1, :] += dgain
             after(l)
 
-    def send_back(m):
+    def line_up(m):
         for s in range(0, slots, LANES):
             back[m, s : s + LANES, :] = dot(place[m, s : s + LANES, :], grad_ref[m]).astype(BF16)
         pltpu.make_async_copy(back.at[m, here], returned.at[m, here], recv_sem.at[3 + m]).start()
-        scatter_to(
-            shards - 1,
-            device,
-            lambda k: back.at[m, pl.ds(pl.multiple_of(index(k) * CAP, CAP), CAP)],
+
+    def send_back(m, rounds=None):
+        to_emb(
+            sizes,
+            lambda peer: back.at[m, pl.ds(pl.multiple_of(peer * CAP, CAP), CAP)],
             returned.at[m, here],
             send_sem.at[3 + m],
             recv_sem.at[3 + m],
+            rounds,
         )
 
     theirs = pl.ds(pl.multiple_of((1 - c) * half, half), half)
     ours = pl.ds(pl.multiple_of(c * half, half), half)
 
-    def halves(l):
-        s0[l] = dweight_ref[l, theirs, :].astype(BF16)
-        if l % deep == 0:
-            b = l // deep
-            remote(s0.at[pl.ds(l, deep)], r0.at[pl.ds(l, deep)], wsend.at[0, b], wrecv.at[0, b], sibling).start()
+
+    def of(b):
+        return pl.ds(sets[b][0], sets[b][1])
+
+    def piece(b, p, start):
+        return (
+            of(b),
+            pl.ds(pl.multiple_of(start + (p // 2) * high, 16), high),
+            pl.ds(pl.multiple_of(lax.rem(p, 2) * LANES, LANES), LANES),
+        )
+
+    def added(ref, size):
+        total = ref[0].astype(F32)
+        for k in range(1, size):
+            total = total + ref[k].astype(F32)
+        return total
+
+    def pair(b):
+        for l in range(sets[b][0], sum(sets[b])):
+            s0[l] = dweight_ref[l, theirs, :].astype(BF16)
+        remote(s0.at[of(b)], r0.at[of(b)], wsend.at[0, b], wrecv.at[0, b], sibling).start()
+
+    def across(b):
+        whole(r0.at[of(b)], wrecv.at[0, b])
+        for l in range(sets[b][0], sum(sets[b])):
+            s1[l] = (dweight_ref[l, ours, :] + r0[l].astype(F32)).astype(BF16)
+        pltpu.make_async_copy(s1.at[piece(b, p_me, 0)], r1[b].at[p_me], wrecv.at[1, b]).start()
+        scatter_to(
+            plane - 1, p_device, lambda k: s1.at[piece(b, p_index(k), 0)], r1[b].at[p_me], wsend.at[1, b], wrecv.at[1, b]
+        )
+
+    def along(b):
+        whole(r1[b], wrecv.at[1, b])
+        total = added(r1[b], plane)
+        total = total.reshape(total.shape[0] * total.shape[1], LANES)
+        per = total.shape[0] // z_size
+        for k in range(z_size):
+            s2[b][k, 0:per, :] = total[k * per : (k + 1) * per].astype(BF16)
+        pltpu.make_async_copy(s2[b].at[z], r2[b].at[z], wrecv.at[2, b]).start()
+        scatter_to(z_size - 1, z_device, lambda k: s2[b].at[z_index(k)], r2[b].at[z], wsend.at[2, b], wrecv.at[2, b])
+
+    def told(b):
+        whole(r2[b], wrecv.at[2, b])
+        t2[b][z] = added(r2[b], z_size).astype(BF16)
+        scatter_to(z_size - 1, z_device, lambda k: t2[b].at[z], t2[b].at[z], wsend.at[5, b], wrecv.at[5, b])
+
+    def across_back(b):
+        whole(t2[b].at[pl.ds(0, z_size - 1)], wrecv.at[5, b])
+        per = r3[b].shape[0] * r3[b].shape[1] // z_size
+        total = jnp.concatenate([t2[b][k, 0:per, :].astype(F32) for k in range(z_size)], axis=0)
+        r3[b][...] = total.reshape(r3[b].shape).astype(BF16)
+        spot = weight_out.at[piece(b, p_me, c * half)]
+        pltpu.make_async_copy(r3[b], spot, wrecv.at[3, b]).start()
+        scatter_to(plane - 1, p_device, lambda k: r3[b], spot, wsend.at[3, b], wrecv.at[3, b])
+
+    def pair_back(b):
+        done = weight_out.at[of(b), ours]
+        whole(done, wrecv.at[3, b])
+        remote(done, done, wsend.at[4, b], wrecv.at[4, b], sibling).start()
+
+    way = [pair, across, along, told, across_back, pair_back]
+
+    def advance(*steps):
+        for b, phase in steps:
+            way[phase](b)
+
+    def gain_axis(phase, me, size, to, source, ref):
+        ref[me] = source
+        scatter_to(size - 1, to, lambda k: ref.at[me], ref.at[me], wsend.at[phase, count], wrecv.at[phase, count])
+
+    def gain_sum(phase, size, ref):
+        whole(ref.at[pl.ds(0, size - 1)], wrecv.at[phase, count])
+        return added(ref, size)
+
+    def during(l):
+        for step in DURING.get(layers - 1 - l, ()):
+            advance(step)
 
     whole(fetched.at[0], recv_sem.at[1])
     forward(0)
     g0[0] = jnp.zeros_like(g0[0])
     backward(0, lambda l: None)
+    line_up(0)
     send_back(0)
     whole(fetched.at[1], recv_sem.at[2])
     forward(1)
-    backward(1, halves)
-    send_back(1)
-
-    last = batches
-    gain_pair = remote(g0.at[0], g0.at[1], wsend.at[0, last], wrecv.at[0, last], sibling)
+    backward(1, during)
+
+    gain_pair = remote(g0.at[0], g0.at[1], wsend.at[0, count], wrecv.at[0, count], sibling)
     gain_pair.start()
-
-    def piece(p):
-        return (
-            pl.ds(pl.multiple_of((p // 2) * high, 16), high),
-            pl.ds(pl.multiple_of(lax.rem(p, 2) * LANES, LANES), LANES),
-        )
-
-    def out_piece(p):
-        return (
-            pl.ds(pl.multiple_of(c * half + (p // 2) * high, 16), high),
-            pl.ds(pl.multiple_of(lax.rem(p, 2) * LANES, LANES), LANES),
-        )
-
-    order = list(reversed(range(batches)))
-    for b in order:
-        at = pl.ds(b * deep, deep)
-        whole(r0.at[at], wrecv.at[0, b])
-        for l in range(b * deep, (b + 1) * deep):
-            s1[l] = (dweight_ref[l, ours, :] + r0[l].astype(F32)).astype(BF16)
-        pltpu.make_async_copy(s1.at[(at, *piece(p_me))], r1.at[b, p_me], wrecv.at[1, b]).start()
-        scatter_to(
-            plane - 1,
-            p_device,
-            lambda k, at=at: s1.at[(at, *piece(p_index(k)))],
-            r1.at[b, p_me],
-            wsend.at[1, b],
-            wrecv.at[1, b],
-        )
-    gain_pair.wait_recv()
-    g1[p_me] = g0[0] + g0[1]
-    scatter_to(plane - 1, p_device, lambda k: g1.at[p_me], g1.at[p_me], wsend.at[1, last], wrecv.at[1, last])
-    for b in order:
-        whole(r1.at[b], wrecv.at[1, b])
-        total = r1[b, 0].astype(F32)
-        for p in range(1, plane):
-            total = total + r1[b, p].astype(F32)
-        r2[b, z] = total.astype(BF16)
-        scatter_to(z_size - 1, z_device, lambda k, b=b: r2.at[b, z], r2.at[b, z], wsend.at[2, b], wrecv.at[2, b])
-    whole(g1.at[pl.ds(0, plane - 1)], wrecv.at[1, last])
-    whole(g1.at[pl.ds(0, plane - 1)], wsend.at[1, last])
-    total = g1[0]
-    for p in range(1, plane):
-        total = total + g1[p]
-    g2[z] = total
-    scatter_to(z_size - 1, z_device, lambda k: g2.at[z], g2.at[z], wsend.at[2, last], wrecv.at[2, last])
+    line_up(1)
+    parts = len(AFTER)
+    cuts = [2 * y_size * k // parts for k in range(parts + 1)]
+    for k, steps in enumerate(AFTER):
+        send_back(1, (cuts[k], cuts[k + 1]))
+        advance(*steps)
+        if k == 0:
+            gain_pair.wait_recv()
+            gain_axis(1, x, x_size, x_device, g0[0] + g0[1], g1)
+        if k == 1:
+            gain_axis(2, y, y_size, y_device, gain_sum(1, x_size, g1), g2)
+        if k == 2:
+            gain_axis(3, z, z_size, z_device, gain_sum(2, y_size, g2), g3)
     whole(returned.at[0], recv_sem.at[3])
-    conv[...] = dot(add[0], returned[0])
-    for b in order:
-        at = pl.ds(b * deep, deep)
-        whole(r2.at[b, pl.ds(0, z_size - 1)], wrecv.at[2, b])
-        total = r2[b, 0].astype(F32)
-        for k in range(1, z_size):
-            total = total + r2[b, k].astype(F32)
-        r3[b] = total.astype(BF16)
-        mine = weight_out.at[(at, *out_piece(p_me))]
-        pltpu.make_async_copy(r3.at[b], mine, wrecv.at[3, b]).start()
-        scatter_to(plane - 1, p_device, lambda k, b=b: r3.at[b], mine, wsend.at[3, b], wrecv.at[3, b])
+    conv[0:rows, :] = dot(add[0], returned[0])
+    advance(*LATE)
 
     share = rows // x_size
     whole(returned.at[1], recv_sem.at[4])
     tsend[...] = (conv[0:rows, :] + dot(add[1], returned[1])).astype(BF16).reshape(x_size, share, width)
     pltpu.make_async_copy(tsend.at[x], trecv.at[x], recv_sem.at[5]).start()
     scatter_to(x_size - 1, x_device, lambda k: tsend.at[x_index(k)], trecv.at[x], send_sem.at[5], recv_sem.at[5])
-
-    for b in order:
-        at = pl.ds(b * deep, deep)
-        done = weight_out.at[at, ours]
-        whole(done, wrecv.at[3, b])
-        remote(done, done, wsend.at[4, b], wrecv.at[4, b], sibling).start()
-
+    advance(*LAST)
     whole(trecv, recv_sem.at[5])
-    total = trecv[0].astype(F32)
-    for k in range(1, x_size):
-        total = total + trecv[k].astype(F32)
-    table_out[x] = total.astype(BF16)
+    table_out[x] = added(trecv, x_size).astype(BF16)
     scatter_to(x_size - 1, x_device, lambda k: table_out.at[x], table_out.at[x], send_sem.at[6], recv_sem.at[6])
 
-    whole(g2.at[pl.ds(0, z_size - 1)], wrecv.at[2, last])
-    total = g2[0]
-    for k in range(1, z_size):
-        total = total + g2[k]
-    gain_out[...] = total[:layers]
-    for b in order:
-        whole(weight_out.at[pl.ds(b * deep, deep), theirs], wrecv.at[4, b])
+    gain_out[...] = gain_sum(3, z_size, g3)
+    for b in range(count):
+        whole(weight_out.at[of(b), theirs], wrecv.at[4, b])
     whole(table_out.at[pl.ds(0, x_size - 1)], recv_sem.at[6])
 
     whole(ask.at[pl.ds(0, shards - 1)], send_sem.at[0])
@@ -403,15 +480,38 @@
         whole(back.at[m, pl.ds(0, slots - CAP)], send_sem.at[3 + m])
     whole(tsend.at[pl.ds(0, x_size - 1)], send_sem.at[5])
     whole(tsend.at[pl.ds(0, x_size - 1)], send_sem.at[6])
-    for b in range(batches):
-        at = pl.ds(b * deep, deep)
-        whole(s0.at[at], wsend.at[0, b])
-        whole(r1.at[b, pl.ds(0, plane - 1)], wsend.at[1, b])
-        whole(r2.at[b, pl.ds(0, z_size - 1)], wsend.at[2, b])
-        whole(r1.at[b, pl.ds(0, plane - 1)], wsend.at[3, b])
-        whole(weight_out.at[at, ours], wsend.at[4, b])
+    for b in range(count):
+        whole(s0.at[of(b)], wsend.at[0, b])
+        whole(r1[b].at[pl.ds(0, plane - 1)], wsend.at[1, b])
+        whole(s2[b].at[pl.ds(0, z_size - 1)], wsend.at[2, b])
+        whole(t2[b].at[pl.ds(0, z_size - 1)], wsend.at[5, b])
+        whole(r1[b].at[pl.ds(0, plane - 1)], wsend.at[3, b])
+        whole(weight_out.at[of(b), ours], wsend.at[4, b])
     gain_pair.wait_send()
-    whole(g2.at[pl.ds(0, z_size - 1)], wsend.at[2, last])
+    whole(g1.at[pl.ds(0, x_size - 1)], wsend.at[1, count])
+    whole(g2.at[pl.ds(0, y_size - 1)], wsend.at[2, count])
+    whole(g3.at[pl.ds(0, z_size - 1)], wsend.at[3, count])
+
+
+def scale_kernel(scale, weight_ref, gain_ref, table_ref, weight_out, gain_out, table_out,
+                 weight, wide, table, tall, load_sem, store_sem):
+    layers = weight.shape[0]
+    loads = [pltpu.make_async_copy(weight_ref.at[l], weight.at[l], load_sem.at[l]) for l in range(layers)]
+    loads.append(pltpu.make_async_copy(table_ref, table, load_sem.at[layers]))
+    stores = [pltpu.make_async_copy(wide.at[l], weight_out.at[l], store_sem.at[l]) for l in range(layers)]
+    stores.append(pltpu.make_async_copy(tall, table_out, store_sem.at[layers]))
+    for load in loads:
+        load.start()
+    gain_out[...] = gain_ref[...] * scale
+    for l in range(layers):
+        loads[l].wait()
+        wide[l] = weight[l].astype(F32) * scale
+        stores[l].start()
+    loads[layers].wait()
+    tall[...] = table[...].astype(F32)
+    stores[layers].start()
+    for store in stores:
+        store.wait()
 
 
 def body(table, owner, row, conv_weight, gain, upstream):
@@ -421,12 +521,20 @@
     layers, taps, _ = conv_weight.shape
     slots = shards * CAP
     z_size, y_size, _, x_size = plan(shards, seq_axis)
-    plane = x_size * y_size
+    sets = batches_of(layers)
     shape = jax.ShapeDtypeStruct
     dma = pltpu.SemaphoreType.DMA
     half = taps // 2
+    share = rows // x_size
+    plane = x_size * y_size
     high = half // (plane // 2)
-    share = rows // x_size
+    one_z = [(z_size, -(-n * high // z_size // 16) * 16, LANES) for _, n in sets]
+    shapes = (
+        [(plane, n, high, LANES) for _, n in sets]
+        + one_z * 3
+        + [(n, high, LANES) for _, n in sets]
+    )
+    work = [pltpu.VMEM(dims, BF16) for dims in shapes]
     near = pl.BlockSpec(memory_space=pltpu.VMEM)
     far = pl.BlockSpec(memory_space=pl.ANY)
     weight_sum, gain_sum, table_grad = pl.pallas_call(
@@ -465,24 +573,37 @@
             pltpu.VMEM((layers, half, width), BF16),
             pltpu.VMEM((layers, half, width), BF16),
             pltpu.VMEM((layers, half, width), BF16),
-            pltpu.VMEM((2, plane, layers // 2, high, LANES), BF16),
-            pltpu.VMEM((2, z_size, layers // 2, high, LANES), BF16),
-            pltpu.VMEM((2, layers // 2, high, LANES), BF16),
-            pltpu.VMEM((2, 2 * layers, width), F32),
-            pltpu.VMEM((plane, 2 * layers, width), F32),
-            pltpu.VMEM((z_size, 2 * layers, width), F32),
+            pltpu.VMEM((2, layers, width), F32),
+            pltpu.VMEM((x_size, layers, width), F32),
+            pltpu.VMEM((y_size, layers, width), F32),
+            pltpu.VMEM((z_size, layers, width), F32),
             dma((2,)),
             dma((7,)),
             dma((7,)),
-            dma((5, 3)),
-            dma((5, 3)),
+            dma((6, len(sets) + 1)),
+            dma((6, len(sets) + 1)),
+            *work,
         ],
         compiler_params=pltpu.CompilerParams(
             collective_id=0, has_side_effects=True, vmem_limit_bytes=60 * 2**20
         ),
     )(owner.reshape(MB, 1, tokens), row, table, gain, conv_weight, upstream)
     scale = float(MB * tokens * shards * seq_axis) ** (-0.5)
-    return weight_sum.astype(F32) * scale, gain_sum * scale, table_grad.astype(F32).reshape(rows, width)
+    return pl.pallas_call(
+        functools.partial(scale_kernel, scale),
+        out_shape=[shape((layers, taps, width), F32), shape((layers, width), F32), shape((rows, width), F32)],
+        in_specs=[far, near, far],
+        out_specs=[far, near, far],
+        scratch_shapes=[
+            pltpu.VMEM((layers, taps, width), BF16),
+            pltpu.VMEM((layers, taps, width), F32),
+            pltpu.VMEM((rows, width), BF16),
+            pltpu.VMEM((rows, width), F32),
+            dma((layers + 1,)),
+            dma((layers + 1,)),
+        ],
+        compiler_params=pltpu.CompilerParams(vmem_limit_bytes=60 * 2**20),
+    )(weight_sum, gain_sum, table_grad.reshape(rows, width))
 
 
 def solution(mesh):

time: 104 us -> 96.7 us (0.930); the launches traced: 102 us -> 96.2 us
  other arithmetic: 4.82 us -> 0 us
  Pallas kernels: 96.6 us -> 95.4 us
    pallas_call x1, Pallas kernels: 96.6 us -> 91.2 us  [body(): pl.pallas_call(functools.partial(window_kernel, shards, seq_axis, 64), ou...]
    pallas_call x0 -> x1, Pallas kernels: none -> 4.23 us  [body(): pl.pallas_call(functools.partial(scale_kernel, scale), out_shape=[shape((...]
    mul x2 -> x0, other arithmetic: 3.97 us -> none  [the longest x1 3.38 us: body(): weight_sum.astype(F32) * scale]
where the time goes in v3:
time: 96.7 us; the launch traced here: 96.2 us
  Pallas kernels  95.4 us (99%)
    pallas_call x1, Pallas kernels, body(): pl.pallas_call(functools.partial(window_kernel, shards, seq_axis, 64), ou...  91.2 us
    pallas_call x1, Pallas kernels, body(): pl.pallas_call(functools.partial(scale_kernel, scale), out_shape=[shape((...  4.23 us

profile of v3, /device:TPU:4, one launch (start us, length us, event | category | flops | bytes accessed | tf_op | source)
XLA Modules:
  0.0 96.2 jit_solution(2135424242933599255)
XLA Ops:
  0.6 91.2 %shard_map.85 = (bf16[4,768,256]{2,1,0:T(8,128)(2,1)}, f32[4,256]{1,0:T(4,128)}, bf16[4,128,256]{2,1,0:T(8,128)(2,1)}) custom-call(s32[2,1,512]{2,1,0:T(1,128)} %bitcast.3, s32[2,512]{1,0:T(2,128)} %row_ref.1, bf16[512,256]{1,0:T(8,128)(2,1)} %table_ref.1, f32[4,256]{1,0:T(4,128)} %gain_ref.1, f32[4,768,256]{2,1,0:T(8,128)} %weight_hbm.1, ...), custom_call_target="tpu_custom_call" | custom-call | tf_op jit(solution)/shard_map/pallas_call | solution.py:540
  91.8 4.2 %shard_map.86 = (f32[4,768,256]{2,1,0:T(8,128)}, f32[4,256]{1,0:T(4,128)}, f32[512,256]{1,0:T(8,128)}) custom-call(bf16[4,768,256]{2,1,0:T(8,128)(2,1)} %get-tuple-element.6.weight_ref, f32[4,256]{1,0:T(4,128)} %get-tuple-element.7.gain_ref, bf16[512,256]{1,0:T(8,128)(2,1)} %bitcast.2), custom_call_target="tpu_custom_call" | custom-call | tf_op jit(solution)/shard_map/pallas_call | solution.py:592

commit v4 on v3

--- a/solution.py
+++ b/solution.py
@@ -123,15 +123,7 @@
     return owner * CAP + slot, wanted.astype(I32)
 
 
-DURING = {0: [(0, 0)], 1: [(0, 1), (1, 0)], 2: [(1, 1), (2, 0)], 3: [(2, 1), (3, 0), (0, 2)]}
-AFTER = [
-    [(3, 1), (1, 2)],
-    [(2, 2), (0, 3)],
-    [(3, 2), (1, 3), (2, 3)],
-    [(0, 4), (3, 3), (1, 4)],
-]
-LATE = [(2, 4), (3, 4), (0, 5), (1, 5)]
-LAST = [(2, 5), (3, 5)]
+DURING = {0: [(0, 0)], 1: [(0, 1), (1, 0)], 2: [(1, 1), (2, 0)], 3: [(2, 1), (3, 0)]}
 
 
 def batches_of(layers):
@@ -161,7 +153,8 @@
     half = taps // 2
     sets = batches_of(layers)
     count = len(sets)
-    r1, s2, r2, t2, r3 = (work[k * count : (k + 1) * count] for k in range(5))
+    r1 = work[:count]
+    r3, s2, r2, t2 = (work[count + 2 * k : count + 2 * k + 2] for k in range(4))
     plane = x_size * y_size
     p_me = x * y_size + y
     high = half // (plane // 2)
@@ -241,6 +234,8 @@
         for g in range(groups):
             hot = jnp.where(iota((LANES, rows), 1).astype(F32) == tall[:, g : g + 1], 1.0, 0.0).astype(BF16)
             serve[m, g * LANES : (g + 1) * LANES, :] = dot(hot, table_ref[...]).astype(BF16)
+        if m:
+            whole(serve.at[0, pl.ds(0, slots - CAP)], send_sem.at[1])
         pltpu.make_async_copy(serve.at[m, here], fetched.at[m, here], recv_sem.at[1 + m]).start()
         to_emb(
             sizes,
@@ -356,9 +351,9 @@
     def of(b):
         return pl.ds(sets[b][0], sets[b][1])
 
-    def piece(b, p, start):
+    def piece(some, p, start):
         return (
-            of(b),
+            some,
             pl.ds(pl.multiple_of(start + (p // 2) * high, 16), high),
             pl.ds(pl.multiple_of(lax.rem(p, 2) * LANES, LANES), LANES),
         )
@@ -378,41 +373,45 @@
         whole(r0.at[of(b)], wrecv.at[0, b])
         for l in range(sets[b][0], sum(sets[b])):
             s1[l] = (dweight_ref[l, ours, :] + r0[l].astype(F32)).astype(BF16)
-        pltpu.make_async_copy(s1.at[piece(b, p_me, 0)], r1[b].at[p_me], wrecv.at[1, b]).start()
+        pltpu.make_async_copy(s1.at[piece(of(b), p_me, 0)], r1[b].at[p_me], wrecv.at[1, b]).start()
         scatter_to(
-            plane - 1, p_device, lambda k: s1.at[piece(b, p_index(k), 0)], r1[b].at[p_me], wsend.at[1, b], wrecv.at[1, b]
+            plane - 1, p_device, lambda k: s1.at[piece(of(b), p_index(k), 0)], r1[b].at[p_me], wsend.at[1, b], wrecv.at[1, b]
         )
 
-    def along(b):
-        whole(r1[b], wrecv.at[1, b])
-        total = added(r1[b], plane)
-        total = total.reshape(total.shape[0] * total.shape[1], LANES)
-        per = total.shape[0] // z_size
+    deep = layers // 2
+    per_z = deep * high // z_size
+
+    def along(h):
+        parts = []
+        for l in range(h * deep, (h + 1) * deep):
+            b = layers - 1 - l
+            whole(r1[b], wrecv.at[1, b])
+            parts.append(added(r1[b], plane).reshape(high, LANES))
+        total = jnp.concatenate(parts, axis=0)
         for k in range(z_size):
-            s2[b][k, 0:per, :] = total[k * per : (k + 1) * per].astype(BF16)
-        pltpu.make_async_copy(s2[b].at[z], r2[b].at[z], wrecv.at[2, b]).start()
-        scatter_to(z_size - 1, z_device, lambda k: s2[b].at[z_index(k)], r2[b].at[z], wsend.at[2, b], wrecv.at[2, b])
-
-    def told(b):
-        whole(r2[b], wrecv.at[2, b])
-        t2[b][z] = added(r2[b], z_size).astype(BF16)
-        scatter_to(z_size - 1, z_device, lambda k: t2[b].at[z], t2[b].at[z], wsend.at[5, b], wrecv.at[5, b])
-
-    def across_back(b):
-        whole(t2[b].at[pl.ds(0, z_size - 1)], wrecv.at[5, b])
-        per = r3[b].shape[0] * r3[b].shape[1] // z_size
-        total = jnp.concatenate([t2[b][k, 0:per, :].astype(F32) for k in range(z_size)], axis=0)
-        r3[b][...] = total.reshape(r3[b].shape).astype(BF16)
-        spot = weight_out.at[piece(b, p_me, c * half)]
-        pltpu.make_async_copy(r3[b], spot, wrecv.at[3, b]).start()
-        scatter_to(plane - 1, p_device, lambda k: r3[b], spot, wsend.at[3, b], wrecv.at[3, b])
-
-    def pair_back(b):
-        done = weight_out.at[of(b), ours]
-        whole(done, wrecv.at[3, b])
-        remote(done, done, wsend.at[4, b], wrecv.at[4, b], sibling).start()
-
-    way = [pair, across, along, told, across_back, pair_back]
+            s2[h][k, 0:per_z, :] = total[k * per_z : (k + 1) * per_z].astype(BF16)
+        pltpu.make_async_copy(s2[h].at[z], r2[h].at[z], wrecv.at[2, h]).start()
+        scatter_to(z_size - 1, z_device, lambda k: s2[h].at[z_index(k)], r2[h].at[z], wsend.at[2, h], wrecv.at[2, h])
+
+    def told(h):
+        whole(r2[h], wrecv.at[2, h])
+        t2[h][z] = added(r2[h], z_size).astype(BF16)
+        scatter_to(z_size - 1, z_device, lambda k: t2[h].at[z], t2[h].at[z], wsend.at[5, h], wrecv.at[5, h])
+
+    def across_back(h):
+        whole(t2[h].at[pl.ds(0, z_size - 1)], wrecv.at[5, h])
+        total = jnp.concatenate([t2[h][k, 0:per_z, :].astype(F32) for k in range(z_size)], axis=0)
+        r3[h][...] = total.reshape(deep, high, LANES).astype(BF16)
+        spot = weight_out.at[piece(pl.ds(h * deep, deep), p_me, c * half)]
+        pltpu.make_async_copy(r3[h], spot, wrecv.at[3, h]).start()
+        scatter_to(plane - 1, p_device, lambda k: r3[h], spot, wsend.at[3, h], wrecv.at[3, h])
+
+    def pair_back(h):
+        done = weight_out.at[pl.ds(h * deep, deep), ours]
+        whole(done, wrecv.at[3, h])
+        remote(done, done, wsend.at[4, h], wrecv.at[4, h], sibling).start()
+
+    way = [pair, across]
 
     def advance(*steps):
         for b, phase in steps:
@@ -443,50 +442,56 @@
     gain_pair = remote(g0.at[0], g0.at[1], wsend.at[0, count], wrecv.at[0, count], sibling)
     gain_pair.start()
     line_up(1)
-    parts = len(AFTER)
-    cuts = [2 * y_size * k // parts for k in range(parts + 1)]
-    for k, steps in enumerate(AFTER):
-        send_back(1, (cuts[k], cuts[k + 1]))
-        advance(*steps)
-        if k == 0:
-            gain_pair.wait_recv()
-            gain_axis(1, x, x_size, x_device, g0[0] + g0[1], g1)
-        if k == 1:
-            gain_axis(2, y, y_size, y_device, gain_sum(1, x_size, g1), g2)
-        if k == 2:
-            gain_axis(3, z, z_size, z_device, gain_sum(2, y_size, g2), g3)
+    advance((layers - 1, 1))
+    gain_pair.wait_recv()
+    gain_axis(1, x, x_size, x_device, g0[0] + g0[1], g1)
+    along(1)
+    rounds = 2 * y_size
+    send_back(1, (0, rounds // 2))
+    along(0)
+    told(1)
+    gain_axis(2, y, y_size, y_device, gain_sum(1, x_size, g1), g2)
+    send_back(1, (rounds // 2, rounds * 3 // 4))
     whole(returned.at[0], recv_sem.at[3])
     conv[0:rows, :] = dot(add[0], returned[0])
-    advance(*LATE)
+    told(0)
+    send_back(1, (rounds * 3 // 4, rounds))
+    gain_axis(3, z, z_size, z_device, gain_sum(2, y_size, g2), g3)
+    across_back(1)
+    across_back(0)
 
     share = rows // x_size
     whole(returned.at[1], recv_sem.at[4])
     tsend[...] = (conv[0:rows, :] + dot(add[1], returned[1])).astype(BF16).reshape(x_size, share, width)
     pltpu.make_async_copy(tsend.at[x], trecv.at[x], recv_sem.at[5]).start()
     scatter_to(x_size - 1, x_device, lambda k: tsend.at[x_index(k)], trecv.at[x], send_sem.at[5], recv_sem.at[5])
-    advance(*LAST)
+    pair_back(1)
     whole(trecv, recv_sem.at[5])
     table_out[x] = added(trecv, x_size).astype(BF16)
     scatter_to(x_size - 1, x_device, lambda k: table_out.at[x], table_out.at[x], send_sem.at[6], recv_sem.at[6])
 
+    pair_back(0)
     gain_out[...] = gain_sum(3, z_size, g3)
-    for b in range(count):
-        whole(weight_out.at[of(b), theirs], wrecv.at[4, b])
+    for h in range(2):
+        whole(weight_out.at[pl.ds(h * deep, deep), theirs], wrecv.at[4, h])
     whole(table_out.at[pl.ds(0, x_size - 1)], recv_sem.at[6])
 
     whole(ask.at[pl.ds(0, shards - 1)], send_sem.at[0])
     for m in range(MB):
-        whole(serve.at[m, pl.ds(0, slots - CAP)], send_sem.at[1 + m])
+        if m:
+            whole(serve.at[m, pl.ds(0, slots - CAP)], send_sem.at[1 + m])
         whole(back.at[m, pl.ds(0, slots - CAP)], send_sem.at[3 + m])
     whole(tsend.at[pl.ds(0, x_size - 1)], send_sem.at[5])
     whole(tsend.at[pl.ds(0, x_size - 1)], send_sem.at[6])
     for b in range(count):
         whole(s0.at[of(b)], wsend.at[0, b])
         whole(r1[b].at[pl.ds(0, plane - 1)], wsend.at[1, b])
-        whole(s2[b].at[pl.ds(0, z_size - 1)], wsend.at[2, b])
-        whole(t2[b].at[pl.ds(0, z_size - 1)], wsend.at[5, b])
-        whole(r1[b].at[pl.ds(0, plane - 1)], wsend.at[3, b])
-        whole(weight_out.at[of(b), ours], wsend.at[4, b])
+    for h in range(2):
+        for _ in range(deep):
+            whole(r1[0].at[pl.ds(0, plane - 1)], wsend.at[3, h])
+        whole(weight_out.at[pl.ds(h * deep, deep), ours], wsend.at[4, h])
+        whole(s2[h].at[pl.ds(0, z_size - 1)], wsend.at[2, h])
+        whole(t2[h].at[pl.ds(0, z_size - 1)], wsend.at[5, h])
     gain_pair.wait_send()
     whole(g1.at[pl.ds(0, x_size - 1)], wsend.at[1, count])
     whole(g2.at[pl.ds(0, y_size - 1)], wsend.at[2, count])
@@ -528,12 +533,8 @@
     share = rows // x_size
     plane = x_size * y_size
     high = half // (plane // 2)
-    one_z = [(z_size, -(-n * high // z_size // 16) * 16, LANES) for _, n in sets]
-    shapes = (
-        [(plane, n, high, LANES) for _, n in sets]
-        + one_z * 3
-        + [(n, high, LANES) for _, n in sets]
-    )
+    one_z = (z_size, -(-(layers // 2) * high // z_size // 16) * 16, LANES)
+    shapes = [(plane, n, high, LANES) for _, n in sets] + [(layers // 2, high, LANES)] * 2 + [one_z] * 6
     work = [pltpu.VMEM(dims, BF16) for dims in shapes]
     near = pl.BlockSpec(memory_space=pltpu.VMEM)
     far = pl.BlockSpec(memory_space=pl.ANY)

time: 96.7 us -> 95.5 us (0.988)
  no operation moved by 1% of the time
where the time goes in v4:
time: 95.5 us; the launch traced here: 95.4 us
  Pallas kernels  94.6 us (99%)
    pallas_call x1, Pallas kernels, body(): pl.pallas_call(functools.partial(window_kernel, shards, seq_axis, 64), ou...  90.4 us
    pallas_call x1, Pallas kernels, body(): pl.pallas_call(functools.partial(scale_kernel, scale), out_shape=[shape((...  4.23 us

profile of v4, /device:TPU:4, one launch (start us, length us, event | category | flops | bytes accessed | tf_op | source)
XLA Modules:
  0.0 95.4 jit_solution(6367887224952542019)
XLA Ops:
  0.6 90.4 %shard_map.85 = (bf16[4,768,256]{2,1,0:T(8,128)(2,1)}, f32[4,256]{1,0:T(4,128)}, bf16[4,128,256]{2,1,0:T(8,128)(2,1)}) custom-call(s32[2,1,512]{2,1,0:T(1,128)} %bitcast.3, s32[2,512]{1,0:T(2,128)} %row_ref.1, bf16[512,256]{1,0:T(8,128)(2,1)} %table_ref.1, f32[4,256]{1,0:T(4,128)} %gain_ref.1, f32[4,768,256]{2,1,0:T(8,128)} %weight_hbm.1, ...), custom_call_target="tpu_custom_call" | custom-call | tf_op jit(solution)/shard_map/pallas_call | solution.py:541
  91.0 4.2 %shard_map.86 = (f32[4,768,256]{2,1,0:T(8,128)}, f32[4,256]{1,0:T(4,128)}, f32[512,256]{1,0:T(8,128)}) custom-call(bf16[4,768,256]{2,1,0:T(8,128)(2,1)} %get-tuple-element.6.weight_ref, f32[4,256]{1,0:T(4,128)} %get-tuple-element.7.gain_ref, bf16[512,256]{1,0:T(8,128)(2,1)} %bitcast.2), custom_call_target="tpu_custom_call" | custom-call | tf_op jit(solution)/shard_map/pallas_call | solution.py:593

commit v5 on v4

--- a/solution.py
+++ b/solution.py
@@ -498,25 +498,10 @@
     whole(g3.at[pl.ds(0, z_size - 1)], wsend.at[3, count])
 
 
-def scale_kernel(scale, weight_ref, gain_ref, table_ref, weight_out, gain_out, table_out,
-                 weight, wide, table, tall, load_sem, store_sem):
-    layers = weight.shape[0]
-    loads = [pltpu.make_async_copy(weight_ref.at[l], weight.at[l], load_sem.at[l]) for l in range(layers)]
-    loads.append(pltpu.make_async_copy(table_ref, table, load_sem.at[layers]))
-    stores = [pltpu.make_async_copy(wide.at[l], weight_out.at[l], store_sem.at[l]) for l in range(layers)]
-    stores.append(pltpu.make_async_copy(tall, table_out, store_sem.at[layers]))
-    for load in loads:
-        load.start()
+def scale_kernel(scale, weight_ref, gain_ref, table_ref, weight_out, gain_out, table_out):
+    weight_out[...] = weight_ref[...].astype(F32) * scale
     gain_out[...] = gain_ref[...] * scale
-    for l in range(layers):
-        loads[l].wait()
-        wide[l] = weight[l].astype(F32) * scale
-        stores[l].start()
-    loads[layers].wait()
-    tall[...] = table[...].astype(F32)
-    stores[layers].start()
-    for store in stores:
-        store.wait()
+    table_out[...] = table_ref[...].astype(F32)
 
 
 def body(table, owner, row, conv_weight, gain, upstream):
@@ -590,19 +575,17 @@
         ),
     )(owner.reshape(MB, 1, tokens), row, table, gain, conv_weight, upstream)
     scale = float(MB * tokens * shards * seq_axis) ** (-0.5)
+    halves = [
+        pl.BlockSpec((layers // 2, taps, width), lambda k: (k, 0, 0)),
+        pl.BlockSpec((layers, width), lambda k: (0, 0)),
+        pl.BlockSpec((rows // 2, width), lambda k: (k, 0)),
+    ]
     return pl.pallas_call(
         functools.partial(scale_kernel, scale),
+        grid=(2,),
         out_shape=[shape((layers, taps, width), F32), shape((layers, width), F32), shape((rows, width), F32)],
-        in_specs=[far, near, far],
-        out_specs=[far, near, far],
-        scratch_shapes=[
-            pltpu.VMEM((layers, taps, width), BF16),
-            pltpu.VMEM((layers, taps, width), F32),
-            pltpu.VMEM((rows, width), BF16),
-            pltpu.VMEM((rows, width), F32),
-            dma((layers + 1,)),
-            dma((layers + 1,)),
-        ],
+        in_specs=halves,
+        out_specs=halves,
         compiler_params=pltpu.CompilerParams(vmem_limit_bytes=60 * 2**20),
     )(weight_sum, gain_sum, table_grad.reshape(rows, width))
 

time: 95.5 us -> 94.2 us (0.986)
  Pallas kernels: 94.6 us -> 93.5 us
    pallas_call x1, Pallas kernels: 4.23 us -> 3.09 us  [body(): pl.pallas_call(functools.partial(scale_kernel, scale), grid=(2,), out_sha...]
where the time goes in v5:
time: 94.2 us; the launch traced here: 94.1 us
  Pallas kernels  93.5 us (99%)
    pallas_call x1, Pallas kernels, body(): pl.pallas_call(functools.partial(window_kernel, shards, seq_axis, 64), ou...  90.4 us
    pallas_call x1, Pallas kernels, body(): pl.pallas_call(functools.partial(scale_kernel, scale), grid=(2,), out_sha...  3.09 us

profile of v5, /device:TPU:4, one launch (start us, length us, event | category | flops | bytes accessed | tf_op | source)
XLA Modules:
  0.0 94.1 jit_solution(14491316371104803841)
XLA Ops:
  0.6 90.4 %shard_map.85 = (bf16[4,768,256]{2,1,0:T(8,128)(2,1)}, f32[4,256]{1,0:T(4,128)}, bf16[4,128,256]{2,1,0:T(8,128)(2,1)}) custom-call(s32[2,1,512]{2,1,0:T(1,128)} %bitcast.3, s32[2,512]{1,0:T(2,128)} %row_ref.1, bf16[512,256]{1,0:T(8,128)(2,1)} %table_ref.1, f32[4,256]{1,0:T(4,128)} %gain_ref.1, f32[4,768,256]{2,1,0:T(8,128)} %weight_hbm.1, ...), custom_call_target="tpu_custom_call" | custom-call | tf_op jit(solution)/shard_map/pallas_call | solution.py:526
  91.0 3.1 %shard_map.86 = (f32[4,768,256]{2,1,0:T(8,128)}, f32[4,256]{1,0:T(4,128)}, f32[512,256]{1,0:T(8,128)}) custom-call(bf16[4,768,256]{2,1,0:T(8,128)(2,1)} %get-tuple-element.6.weight_ref, f32[4,256]{1,0:T(4,128)} %get-tuple-element.7.gain_ref, bf16[512,256]{1,0:T(8,128)(2,1)} %bitcast.2), custom_call_target="tpu_custom_call" | custom-call | tf_op jit(solution)/shard_map/pallas_call | solution.py:583

commit v6 on v5

--- a/solution.py
+++ b/solution.py
@@ -443,11 +443,11 @@
     gain_pair.start()
     line_up(1)
     advance((layers - 1, 1))
-    gain_pair.wait_recv()
-    gain_axis(1, x, x_size, x_device, g0[0] + g0[1], g1)
     along(1)
     rounds = 2 * y_size
     send_back(1, (0, rounds // 2))
+    gain_pair.wait_recv()
+    gain_axis(1, x, x_size, x_device, g0[0] + g0[1], g1)
     along(0)
     told(1)
     gain_axis(2, y, y_size, y_device, gain_sum(1, x_size, g1), g2)

time: 94.2 us -> 94.2 us (level)
  no operation moved by 1% of the time
where the time goes in v6:
time: 94.2 us; the launch traced here: 94.1 us
  Pallas kernels  93.5 us (99%)
    pallas_call x1, Pallas kernels, body(): pl.pallas_call(functools.partial(window_kernel, shards, seq_axis, 64), ou...  90.4 us
    pallas_call x1, Pallas kernels, body(): pl.pallas_call(functools.partial(scale_kernel, scale), grid=(2,), out_sha...  3.09 us

profile of v6, /device:TPU:4, one launch (start us, length us, event | category | flops | bytes accessed | tf_op | source)
XLA Modules:
  0.0 94.1 jit_solution(16269046350342998101)
XLA Ops:
  0.6 90.4 %shard_map.85 = (bf16[4,768,256]{2,1,0:T(8,128)(2,1)}, f32[4,256]{1,0:T(4,128)}, bf16[4,128,256]{2,1,0:T(8,128)(2,1)}) custom-call(s32[2,1,512]{2,1,0:T(1,128)} %bitcast.3, s32[2,512]{1,0:T(2,128)} %row_ref.1, bf16[512,256]{1,0:T(8,128)(2,1)} %table_ref.1, f32[4,256]{1,0:T(4,128)} %gain_ref.1, f32[4,768,256]{2,1,0:T(8,128)} %weight_hbm.1, ...), custom_call_target="tpu_custom_call" | custom-call | tf_op jit(solution)/shard_map/pallas_call | solution.py:526
  91.0 3.1 %shard_map.86 = (f32[4,768,256]{2,1,0:T(8,128)}, f32[4,256]{1,0:T(4,128)}, f32[512,256]{1,0:T(8,128)}) custom-call(bf16[4,768,256]{2,1,0:T(8,128)(2,1)} %get-tuple-element.6.weight_ref, f32[4,256]{1,0:T(4,128)} %get-tuple-element.7.gain_ref, bf16[512,256]{1,0:T(8,128)(2,1)} %bitcast.2), custom_call_target="tpu_custom_call" | custom-call | tf_op jit(solution)/shard_map/pallas_call | solution.py:583
